TPU v7x, 256 devices: a whole 4x4x8 slice. The times are simulated.
256 devices in a mesh: span: 64 (over z, x, core), cross: 4 (over y).
Axes of the slice: x: 4, y: 4, z: 8, core: 2. Of those that a mesh axis runs over, the one named last changes fastest.
Arguments:
- populations: bfloat16 [19, 1024, 128, 128], P(None, 'span', 'cross'), may hold values from 0.2 to 1.8
- cell_index: int32 [32768, 8], P(('span', 'cross')), may hold values from 0 to 65535
- marker_weight: float32 [32768, 8], P(('span', 'cross')), may hold values from 0 to 0.25
- segment_id: int32 [32768], P(('span', 'cross')), may hold values from 0 to 2047, as said below
Outputs:
- populations_next: bfloat16 [19, 1024, 128, 128], P(None, 'span', 'cross')
- eddy_coeff: float32 [128, 128], P('cross')
- segment_force: float32 [3, 2048], P(None, ('span', 'cross'))
Inputs may be any that keep to these rules, and one draw needn't show every extreme that they name: cell_index addresses a cell of the block of the device that holds the marker, flat in the order (span, crossflow, stream) of that 16 x 32 x 128 block. `segment_id`: segments are owned 8 to a device in device order (span slowest); a marker's segment may be owned by any device.
All inputs are finite; a program needn't handle non-finite values.
Results may differ from a plain program's by a relative error of at most 0.0019.
The roundings to bfloat16 on the way count: a program that leaves them out, or rounds other values in their place, can miss the bound.
Values may be sent and summed in bfloat16 or wider, within the bound.
A program may use at most 128 MiB of HBM per device.

v0:
```python
import jax
import jax.numpy as jnp
from jax import lax
from jax.sharding import PartitionSpec as P

SEG_DEV = 8


eps_sum = 1e-06
base_visc = 0.005


def extended(block, sides, width):
    for axis, dim in sides:
        count = lax.axis_size(axis)
        forward = [(i, i + 1) for i in range(count - 1)]
        forward.append((count - 1, 0))
        backward = [(target, source) for source, target in forward]
        low = lax.ppermute(
            lax.slice_in_dim(block, block.shape[dim] - width, None, axis=dim), axis, forward
        )
        high = lax.ppermute(lax.slice_in_dim(block, 0, width, axis=dim), axis, backward)
        block = jnp.concatenate([low, block, high], axis=dim)
    return block


def lattice_tables():
    velocities = [
        [0, 0, 0],
        [1, 0, 0],
        [-1, 0, 0],
        [0, 1, 0],
        [0, -1, 0],
        [0, 0, 1],
        [0, 0, -1],
        [1, 1, 0],
        [-1, -1, 0],
        [1, -1, 0],
        [-1, 1, 0],
        [1, 0, 1],
        [-1, 0, -1],
        [1, 0, -1],
        [-1, 0, 1],
        [0, 1, 1],
        [0, -1, -1],
        [0, 1, -1],
        [0, -1, 1],
    ]
    weights = [1.0 / 3.0] + [1.0 / 18.0] * 6 + [1.0 / 36.0] * 12
    return (velocities, weights)


def inner_product(first, second):
    return sum((first[index] * second[index] for index in range(19)))


def relax_tables():
    velocities, weights = lattice_tables()
    along_x = [float(entry[0]) for entry in velocities]
    along_y = [float(entry[1]) for entry in velocities]
    along_z = [float(entry[2]) for entry in velocities]
    polynomials = []
    for index in range(19):
        cx, cy, cz = (along_x[index], along_y[index], along_z[index])
        square = cx * cx + cy * cy + cz * cz
        normal_x = 3.0 * cx * cx - square
        normal_yz = cy * cy - cz * cz
        polynomials.append(
            [
                1.0,
                square,
                square * square,
                cx,
                cx * square,
                cy,
                cy * square,
                cz,
                cz * square,
                normal_x,
                normal_x * square,
                normal_yz,
                normal_yz * square,
                cx * cy,
                cy * cz,
                cx * cz,
                cx * (cy * cy - cz * cz),
                cy * (cz * cz - cx * cx),
                cz * (cx * cx - cy * cy),
            ]
        )
    ortho_rows = []
    for moment in range(19):
        vector = [polynomials[index][moment] for index in range(19)]
        for prior in ortho_rows:
            factor = inner_product(vector, prior) / inner_product(prior, prior)
            vector = [vector[index] - factor * prior[index] for index in range(19)]
        ortho_rows.append(vector)
    norms = [inner_product(row_vec, row_vec) for row_vec in ortho_rows]
    fixed = [
        0.0,
        1.19,
        1.4,
        0.0,
        1.2,
        0.0,
        1.2,
        0.0,
        1.2,
        0.0,
        1.4,
        0.0,
        1.4,
        0.0,
        0.0,
        0.0,
        1.98,
        1.98,
        1.98,
    ]
    shear = [1.0 if moment in (9, 11, 13, 14, 15) else 0.0 for moment in range(19)]

    def build(rates):
        return [
            [
                sum(
                    (
                        ortho_rows[moment][outer]
                        / norms[moment]
                        * rates[moment]
                        * ortho_rows[moment][inner]
                        for moment in range(19)
                    )
                )
                for inner in range(19)
            ]
            for outer in range(19)
        ]

    return (build(fixed), build(shear))


def moment_basis():
    velocities, weights = lattice_tables()
    return [[1.0] * 19] + [[float(entry[dim]) for entry in velocities] for dim in range(3)]


def moments(pops):
    basis = jnp.asarray(moment_basis(), jnp.bfloat16)
    sums = jnp.dot(basis, pops.reshape(19, -1), preferred_element_type=jnp.float32)
    density = sums[0]
    return (density, sums[1:] / density)


def collide(pops, density, velocity, rate):
    velocities, weights = lattice_tables()
    fixed_mat, shear_mat = relax_tables()
    flat = pops.reshape(19, -1).astype(jnp.float32)
    along = jnp.dot(jnp.asarray(velocities, jnp.float32), velocity, precision=lax.Precision.HIGHEST)
    speed = jnp.sum(velocity * velocity, axis=0)
    equil = (
        jnp.asarray(weights, jnp.float32)[:, None]
        * density
        * (1.0 + 3.0 * along + 4.5 * along * along - 1.5 * speed)
    )
    offeq = flat - equil
    relaxed = jnp.dot(jnp.asarray(fixed_mat, jnp.float32), offeq, precision=lax.Precision.HIGHEST)
    sheared = jnp.dot(jnp.asarray(shear_mat, jnp.float32), offeq, precision=lax.Precision.HIGHEST)
    post = flat - relaxed - rate.reshape(-1) * sheared
    return post.astype(jnp.bfloat16).reshape(pops.shape)


def crop(array):
    return array[..., 1:-1, 1:-1, :]


def diff_z(array):
    return 0.5 * (array[..., 2:, 1:-1, :] - array[..., :-2, 1:-1, :])


def diff_y(array):
    return 0.5 * (array[..., 1:-1, 2:, :] - array[..., 1:-1, :-2, :])


def diff_x(array):
    return crop(0.5 * (jnp.roll(array, -1, -1) - jnp.roll(array, 1, -1)))


def smooth(array):
    first = 0.25 * (array[..., :-2, :, :] + 2.0 * array[..., 1:-1, :, :] + array[..., 2:, :, :])
    second = 0.25 * (first[..., :-2, :] + 2.0 * first[..., 1:-1, :] + first[..., 2:, :])
    return 0.25 * (jnp.roll(second, 1, -1) + 2.0 * second + jnp.roll(second, -1, -1))


def strain(field):
    grad_x, grad_y, grad_z = (diff_x(field), diff_y(field), diff_z(field))
    parts = jnp.stack(
        [
            grad_x[0],
            grad_y[1],
            grad_z[2],
            0.5 * (grad_y[0] + grad_x[1]),
            0.5 * (grad_z[0] + grad_x[2]),
            0.5 * (grad_z[1] + grad_y[2]),
        ]
    )
    magnitude = jnp.sqrt(
        2.0 * (jnp.sum(parts[:3] ** 2, axis=0) + 2.0 * jnp.sum(parts[3:] ** 2, axis=0))
    )
    return (parts, magnitude)


def pair_products(field):
    return jnp.stack(
        [
            field[0] * field[0],
            field[1] * field[1],
            field[2] * field[2],
            field[0] * field[1],
            field[0] * field[2],
            field[1] * field[2],
        ]
    )


def germano(padded):
    strain_one, mag_one = strain(padded)
    hat_ss = smooth(mag_one * strain_one)
    vel_hat = smooth(padded)
    strain_hat, mag_hat = strain(vel_hat)
    hat_prods = smooth(pair_products(crop(padded)))
    leonard = hat_prods - pair_products(crop(vel_hat))
    model = 2.0 * (hat_ss - 4.0 * mag_hat * strain_hat)
    counts = jnp.asarray([1.0, 1.0, 1.0, 2.0, 2.0, 2.0], jnp.float32)[:, None, None, None]
    plane_lm = jnp.sum(counts * leonard * model, axis=(0, 1))
    plane_mm = jnp.sum(counts * model * model, axis=(0, 1))
    return (plane_lm, plane_mm, crop(mag_one))


def stream(rimmed):
    velocities, weights = lattice_tables()
    depth, width = (rimmed.shape[1] - 2, rimmed.shape[2] - 2)
    planes = []
    for index in range(19):
        shift_x, shift_y, shift_z = (
            velocities[index][0],
            velocities[index][1],
            velocities[index][2],
        )
        piece = rimmed[
            index, 1 - shift_z : 1 - shift_z + depth, 1 - shift_y : 1 - shift_y + width, :
        ]
        planes.append(jnp.roll(piece, shift_x, axis=-1))
    return jnp.stack(planes)


def local(populations, cell_index, marker_weight, segment_id):
    block_shape = populations.shape[1:]
    density, velocity = moments(populations)
    field = velocity.reshape((3,) + block_shape)
    padded = extended(field, (("span", 1), ("cross", 2)), 2)
    plane_lm, plane_mm, magnitude = germano(padded)
    total_lm, total_mm = lax.psum((plane_lm, plane_mm), "span")
    eddy_coeff = jnp.maximum(total_lm / (total_mm + eps_sum), 0.0)
    rate = 1.0 / (0.5 + 3.0 * (base_visc + eddy_coeff * magnitude))
    post = collide(populations, density, velocity, rate)
    rimmed = extended(post, (("span", 1), ("cross", 2)), 1)
    populations_next = stream(rimmed)
    momentum = jnp.dot(
        jnp.asarray(moment_basis()[1:], jnp.bfloat16),
        populations_next.reshape(19, -1),
        preferred_element_type=jnp.float32,
    )
    picked = momentum[:, cell_index]
    force = -jnp.sum(marker_weight * picked, axis=-1)
    segments_all = SEG_DEV * lax.axis_size("span") * lax.axis_size("cross")
    partial_force = jax.ops.segment_sum(force.T, segment_id, num_segments=segments_all).T
    segment_force = lax.psum_scatter(
        partial_force, ("span", "cross"), scatter_dimension=1, tiled=True
    )
    return (populations_next, eddy_coeff, segment_force)


def solution(mesh):
    in_specs = (
        P(None, "span", "cross", None),
        P(("span", "cross"), None),
        P(("span", "cross"), None),
        P(("span", "cross")),
    )
    out_specs = (P(None, "span", "cross", None), P("cross", None), P(None, ("span", "cross")))
    return jax.shard_map(local, mesh=mesh, in_specs=in_specs, out_specs=out_specs, check_vma=False)
```

profile of v0, /device:TPU:1, one launch (start us, length us, event | category | flops | bytes accessed | tf_op | source)
XLA Modules:
  0.0 458.1 jit_solution(17382106849316097196)
XLA Ops:
  0.6 2.0 pad.88
  2.7 2.0 copy.50
  8.3 2.6 collective-permute-start
  11.6 8.7 %convert_subtract_fusion = f32[19,65536]{1,0:T(8,128)} fusion(bf16[19,65536]{1,0:T(8,128)(2,1)S(1)} %bitcast.117, f32[19,3]{1,0:T(8,128)S(1)} %copy-done.32, f32[65536]{0:T(1024)S(1)} %broadcast_multiply_fusion.4, f32[65536]{0:T(1024)S(1)} %bitcast.143, f32[19]{0:T(128)S(1)} %copy-done.33, f32[4,65536]{1,0:T(4,128)S(1)} %fusion.78), kind=kOutput, calls=%fused_computation.8 | convolution fusion | flops 57475072 | bytes 9974272 | tf_op jit(solution)/shard_map/dot_general | solution.py:158
  20.5 1.2 constant_dynamic-update-slice_fusion.1
  22.7 2.2 collective-permute-start.3
  26.2 3.4 collective-permute-done.2
  29.6 1.4 pad_maximum_fusion
  44.3 2.8 multiply_reduce_fusion
  47.2 248.3 %all-reduce.1 = (f32[32,128]{1,0:T(8,128)}, f32[32,128]{1,0:T(8,128)}) all-reduce(f32[32,128]{1,0:T(8,128)S(1)} %get-tuple-element.19, f32[32,128]{1,0:T(8,128)S(1)} %get-tuple-element.18), channel_id=1, replica_groups=mesh['span'=64,'cross'=4] {'span'}, use_global_device_ids=true, to_apply=%region_6.7 | all-reduce | flops 8192 | bytes 65536 | tf_op jit(solution)/shard_map/psum | solution.py:262
  296.4 7.9 %fusion.1 = f32[19,65536]{1,0:T(8,128)S(1)} fusion(f32[19,65536]{1,0:T(8,128)} %convert_subtract_fusion, f32[19,19]{1,0:T(8,128)} %constant.12.clone, f32[65536]{0:T(1024)S(1)} %bitcast.128), kind=kOutput, calls=%fused_computation.5 | convolution fusion | flops 285147136 | bytes 10225060 | tf_op jit(solution)/shard_map/dot_general | solution.py:167
  304.3 7.8 %fusion.2 = bf16[19,65536]{1,0:T(8,128)(2,1)S(1)} fusion(f32[19,65536]{1,0:T(8,128)S(1)} %fusion.1, f32[19,19]{1,0:T(8,128)S(1)} %copy-done.7, f32[19,65536]{1,0:T(8,128)} %convert_subtract_fusion, bf16[19,65536]{1,0:T(8,128)(2,1)S(1)} %bitcast.118), kind=kOutput, calls=%fused_computation.6 | convolution fusion | flops 288882688 | bytes 14943652 | tf_op jit(solution)/shard_map/dot_general | solution.py:166
  312.1 2.2 slice_reduce_fusion
  315.3 1.8 collective-permute-start.4
  317.1 4.3 collective-permute-start.5
  322.0 2.2 constant_dynamic-update-slice_fusion.21
  324.9 2.7 collective-permute-start.7
  327.6 1.8 collective-permute-done.6
  332.9 1.2 copy-done.8
  335.1 2.8 fusion.33
  337.8 15.9 %copy.48 = f32[3,65536]{0,1:T(8,128)} copy(f32[3,65536]{1,0:T(4,128)S(1)} %fusion.33) | data formatting | bytes 1572864 | tf_op jit(solution)/shard_map/dot_general | solution.py:268
  353.7 13.4 %gather_fusion = f32[1024,3]{1,0:T(8,128)S(1)} fusion(f32[3,65536]{0,1:T(8,128)} %copy.48, s32[1024]{0:T(1024)S(1)} %broadcast_clamp_fusion), kind=kCustom, calls=%fused_computation | custom fusion | bytes 28672 | tf_op jit(solution)/shard_map/gather | solution.py:273
  367.4 1.4 scatter_custom_fusion
  368.8 88.5 %all-reduce = f32[3,2048]{0,1:T(8,128)S(1)} all-reduce(f32[3,2048]{0,1:T(8,128)S(1)} %bitcast.124), channel_id=2, replica_groups=mesh['span'=64,'cross'=4] {'span','cross'}, use_global_device_ids=true, to_apply=%region_11.12.clone | all-reduce | flops 6144 | bytes 49152
  (204 shorter events, 27.7 us)
Async XLA Ops:
  2.7 2.0 copy-start.11
  6.6 4.9 %copy-start.32 = (f32[19,3]{1,0:T(8,128)S(1)}, f32[19,3]{1,0:T(8,128)}, u32[]{:S(2)}) copy-start(f32[19,3]{1,0:T(8,128)} %constant.35.clone) | copy-start | bytes 688
  6.7 4.9 %copy-start.33 = (f32[19]{0:T(128)S(1)}, f32[19]{0:T(128)}, u32[]{:S(2)}) copy-start(f32[19]{0:T(128)} %constant.10.clone) | copy-start | bytes 232
  6.7 0.9 copy-start.2
  8.3 12.2 %collective-permute-start = (f32[3,2,32,128]{3,2,1,0:T(8,128)}, f32[3,2,32,128]{3,2,1,0:T(8,128)S(1)}, u32[]{:S(2)}, u32[]{:S(2)}) collective-permute-start(f32[3,2,32,128]{3,2,1,0:T(8,128)} %get-tuple-element.125), channel_id=1, source_target_pairs={{0,4},{4,8},{8,12},{12,16},{16,20},{20,24},{24,28},{28,32},{32,36}... | collective-permute-start | bytes 294920 | tf_op jit(solution)/shard_map/ppermute | solution.py:19
  10.9 10.8 %collective-permute-start.1 = (f32[3,2,32,128]{3,2,1,0:T(8,128)S(1)}, f32[3,2,32,128]{3,2,1,0:T(8,128)S(1)}, u32[]{:S(2)}, u32[]{:S(2)}) collective-permute-start(f32[3,2,32,128]{3,2,1,0:T(8,128)S(1)} %get-tuple-element.124), channel_id=1, source_target_pairs={{4,0},{8,4},{12,8},{16,12},{20,16},{24,20},{28,24},{32,28},{36,32}... | collective-permute-start | bytes 294920 | tf_op jit(solution)/shard_map/ppermute | solution.py:22
  11.5 8.7 %copy-start.10 = (s32[128,8]{0,1:T(8,128)S(1)}, s32[128,8]{0,1:T(8,128)}, u32[]{:S(2)}) copy-start(s32[128,8]{0,1:T(8,128)} %param.12) | copy-start | bytes 12292
  20.2 5.1 %copy-start.9 = (f32[128,8]{0,1:T(8,128)S(1)}, f32[128,8]{0,1:T(8,128)}, u32[]{:S(2)}) copy-start(f32[128,8]{0,1:T(8,128)} %param.13) | copy-start | bytes 12292
  21.7 0.9 copy-start
  22.7 3.5 collective-permute-start.3
  24.9 4.7 %collective-permute-start.2 = (f32[3,20,2,128]{3,2,1,0:T(2,128)S(1)}, f32[3,20,2,128]{3,2,1,0:T(2,128)S(1)}, u32[]{:S(2)}, u32[]{:S(2)}) collective-permute-start(f32[3,20,2,128]{3,2,1,0:T(2,128)S(1)} %get-tuple-element.118), channel_id=1, source_target_pairs={{0,1},{1,2},{2,3},{3,0},{4,5},{5,6},{6,7},{7,4},{8,9},{9,10},{10,1... | collective-permute-start | bytes 184328 | tf_op jit(solution)/shard_map/ppermute | solution.py:19
  37.1 1.2 copy-start.1
  41.4 1.1 copy-start.3
  42.9 1.4 copy-start.4
  42.9 1.4 copy-start.12
  42.9 1.4 copy-start.13
  296.3 8.0 %copy-start.6 = (f32[32,128]{1,0:T(8,128)}, f32[32,128]{1,0:T(8,128)S(1)}, u32[]{:S(2)}) copy-start(f32[32,128]{1,0:T(8,128)S(1)} %divide_maximum_fusion) | copy-start | bytes 49156
  296.3 7.9 %copy-start.7 = (f32[19,19]{1,0:T(8,128)S(1)}, f32[19,19]{1,0:T(8,128)}, u32[]{:S(2)}) copy-start(f32[19,19]{1,0:T(8,128)} %constant.11.clone) | copy-start | bytes 4336
  315.3 6.6 %collective-permute-start.4 = (bf16[19,1,32,128]{3,2,1,0:T(8,128)(2,1)S(1)}, bf16[19,1,32,128]{3,2,1,0:T(8,128)(2,1)S(1)}, u32[]{:S(2)}, u32[]{:S(2)}) collective-permute-start(bf16[19,1,32,128]{3,2,1,0:T(8,128)(2,1)S(1)} %get-tuple-element.88), channel_id=1, source_target_pairs={{0,4},{4,8},{8,12},{12,16},{16,20},{20,24},{24,28},{28,32},{32,36}... | collective-permute-start | bytes 466952 | tf_op jit(solution)/shard_map/ppermute | solution.py:19
  317.1 7.1 %collective-permute-start.5 = (bf16[19,1,32,128]{3,2,1,0:T(8,128)(2,1)S(1)}, bf16[19,1,32,128]{3,2,1,0:T(8,128)(2,1)S(1)}, u32[]{:S(2)}, u32[]{:S(2)}) collective-permute-start(bf16[19,1,32,128]{3,2,1,0:T(8,128)(2,1)S(1)} %get-tuple-element.87), channel_id=1, source_target_pairs={{4,0},{8,4},{12,8},{16,12},{20,16},{24,20},{28,24},{32,28},{36,32}... | collective-permute-start | bytes 466952 | tf_op jit(solution)/shard_map/ppermute | solution.py:22
  324.6 4.9 %collective-permute-start.6 = (bf16[19,18,1,128]{3,0,2,1:T(8,128)(2,1)S(1)}, bf16[19,18,1,128]{3,0,2,1:T(8,128)(2,1)S(1)}, u32[]{:S(2)}, u32[]{:S(2)}) collective-permute-start(bf16[19,18,1,128]{3,0,2,1:T(8,128)(2,1)S(1)} %copy.42), channel_id=1, source_target_pairs={{0,1},{1,2},{2,3},{3,0},{4,5},{5,6},{6,7},{7,4},{8,9},{9,10},{10,1... | collective-permute-start | bytes 262664 | tf_op jit(solution)/shard_map/ppermute | solution.py:19
  324.9 5.0 %collective-permute-start.7 = (bf16[19,18,1,128]{3,0,2,1:T(8,128)(2,1)S(1)}, bf16[19,18,1,128]{3,0,2,1:T(8,128)(2,1)S(1)}, u32[]{:S(2)}, u32[]{:S(2)}) collective-permute-start(bf16[19,18,1,128]{3,0,2,1:T(8,128)(2,1)S(1)} %copy.44), channel_id=1, source_target_pairs={{1,0},{2,1},{3,2},{0,3},{5,4},{6,5},{7,6},{4,7},{9,8},{10,9},{11,1... | collective-permute-start | bytes 262664 | tf_op jit(solution)/shard_map/ppermute | solution.py:22
  332.7 1.5 copy-start.8
  353.7 13.4 %copy-start.5 = (f32[128,8]{1,0:T(8,128)S(1)}, f32[128,8]{1,0:T(8,128)}, u32[]{:S(2)}) copy-start(f32[128,8]{1,0:T(8,128)} %copy.46) | copy-start | bytes 12292
  (18 other events, 12.9 us)
where the time goes:
time: 467 us; the launch traced here: 458 us
  blocking collectives  337 us (72%)
  local copies, waits for them, and re-layouts  54.4 us (12%)
  matrix products  25.1 us (5%)
  other arithmetic  19.5 us (4%)
  starting transfers between devices  14.7 us (3%)
  waiting for transfers between devices  5.54 us (1%)
    psum x1, blocking collectives, local(): total_lm, total_mm = lax.psum((plane_lm, plane_mm), 'span')  248 us
    unnamed x1, blocking collectives  88.5 us
    dot_general x1, local copies, waits for them, and re-layouts, local(): jnp.dot(jnp.asarray(moment_basis()[1:], jnp.bfloat16), populations_next.r...  15.9 us
    unnamed x84, local copies, waits for them, and re-layouts  15.5 us
    gather x1, local copies, waits for them, and re-layouts, local(): picked = momentum[:, cell_index]  13.4 us
    ppermute x4, starting transfers between devices, extended(): lax.ppermute(lax.slice_in_dim(block, 0, width, axis=dim), axis, backward)  9.8 us
  transfers between devices with their start and end apart: 8, of which 4 were waited for; matrix products, arithmetic and copies ran while one was open for 3% of the time, Pallas kernels for 0%

commit v1 on v0

v1 whole, which is shorter than its diff:
```python
import functools

import jax
import jax.numpy as jnp
from jax import lax
from jax.experimental import pallas as pl
from jax.experimental.pallas import tpu as pltpu
from jax.sharding import PartitionSpec as P

SEG_DEV = 8
MESH = pl.DeviceIdType.MESH
eps_sum = 1e-06
base_visc = 0.005

CHIPS_X = 4
CORES = 2

VELOCITIES = [
    (0, 0, 0),
    (1, 0, 0),
    (-1, 0, 0),
    (0, 1, 0),
    (0, -1, 0),
    (0, 0, 1),
    (0, 0, -1),
    (1, 1, 0),
    (-1, -1, 0),
    (1, -1, 0),
    (-1, 1, 0),
    (1, 0, 1),
    (-1, 0, -1),
    (1, 0, -1),
    (-1, 0, 1),
    (0, 1, 1),
    (0, -1, -1),
    (0, 1, -1),
    (0, -1, 1),
]
ORDER = [18, 5, 11, 14, 15, 3, 7, 10, 17, 6, 12, 13, 16, 4, 8, 9, 0, 1, 2]
PLACE = [ORDER.index(q) for q in range(19)]

ROW = 8
TOP = 48


def add_pairs(f):
    s = [f[2 * i + 1] + f[2 * i + 2] for i in range(9)]
    d = [f[2 * i + 1] - f[2 * i + 2] for i in range(9)]
    return s, d


def tri(low, mid, high):
    return (low + high) + (mid + mid)


def roll_x(a, shift):
    return pltpu.roll(a, shift % a.shape[-1], axis=a.ndim - 1)


def smooth_x(a):
    b = a + roll_x(a, 1)
    return b + roll_x(b, -1)


def strain_of(d):
    exy, exz, eyz = d[0][1] + d[1][0], d[0][2] + d[2][0], d[1][2] + d[2][1]
    diag = d[0][0] * d[0][0] + d[1][1] * d[1][1] + d[2][2] * d[2][2]
    off = exy * exy + exz * exz + eyz * eyz
    mag = jnp.sqrt(0.5 * diag + 0.25 * off)
    return (d[0][0], d[1][1], d[2][2], exy, exz, eyz), mag


PAIRS = [(0, 0), (1, 1), (2, 2), (0, 1), (0, 2), (1, 2)]


def kernel(
    split,
    pops_hbm,
    cell_ref,
    weight_ref,
    seg_ref,
    out_hbm,
    eddy_ref,
    force_ref,
    pops,
    vel,
    mags,
    tmp,
    vtmp,
    vhat,
    filt,
    sums,
    part,
    shear,
    post,
    outv,
    mom,
    pick,
    lanes,
    gath,
    d1s,
    d1r,
    d2,
    d3,
    h1s,
    h1r,
    h2,
    in_sem,
    out_sem,
    v_send,
    v_recv,
    p_send,
    p_recv,
    d1_send,
    d1_recv,
    d2_send,
    d2_recv,
    d3_send,
    d3_recv,
    h1_send,
    h1_recv,
    h2_send,
    h2_recv,
):
    nz, nx, nc, ny = split
    nxc = nx * nc
    nspan = nz * nxc
    cz, cy, cx = pops.shape[1:]
    half = nx // 2
    ng1, ng2 = nz * half, 2 * nc * ny
    s = lax.axis_index("span")
    y = lax.axis_index("cross")
    z, xc = s // nxc, s % nxc
    x, c = xc // nc, xc % nc
    g1 = z * half + x // 2
    g2 = (x % 2) * (nc * ny) + c * ny + y

    def xc_dev(j):
        return (z * nxc + j, y)

    def z_dev(j):
        return (j * nxc + xc, y)

    def g1_dev(j):
        return ((j // half) * nxc + ((j % half) * 2 + x % 2) * nc + c, y)

    def g2_dev(j):
        return (z * nxc + ((x // 2) * 2 + j // (nc * ny)) * nc + (j // ny) % nc, j % ny)

    def near(dz, dy):
        return ((s + dz + nspan) % nspan, (y + dy + ny) % ny)

    sides = [(1, 0), (-1, 0), (0, 1), (0, -1), (1, 1), (1, -1), (-1, 1), (-1, -1)]

    nchunk = in_sem.shape[0]
    step = cz // nchunk

    def fetch(i):
        return pltpu.make_async_copy(
            pops_hbm.at[:, pl.ds(i * step, step)], pops.at[:, pl.ds(i * step, step)], in_sem.at[i]
        )

    for i in range(nchunk):
        fetch(i).start()

    barrier = pltpu.get_barrier_semaphore()

    def greet(dev):
        pl.semaphore_signal(barrier, inc=1, device_id=dev, device_id_type=MESH)

    for dz, dy in sides:
        greet(near(dz, dy))

    def greet_group(me, count, dev):
        def body(k, carry):
            greet(dev((me + k) % count))
            return carry

        lax.fori_loop(1, count, body, 0)

    greet_group(xc, nxc, xc_dev)
    greet_group(z, nz, z_dev)
    greet_group(g1, ng1, g1_dev)
    greet_group(g2, ng2, g2_dev)
    greeted = len(sides) + (nxc - 1) + (nz - 1) + (ng1 - 1) + (ng2 - 1)

    def moments_plane(i, carry):
        f = [pops[q, i].astype(jnp.float32) for q in range(19)]
        sm, d = add_pairs(f)
        density = f[0] + ((sm[0] + sm[1] + sm[2]) + (sm[3] + sm[4] + sm[5]) + (sm[6] + sm[7] + sm[8]))
        jx = d[0] + (d[3] + d[4]) + (d[5] + d[6])
        jy = d[1] + (d[3] - d[4]) + (d[7] + d[8])
        jz = d[2] + (d[5] - d[6]) + (d[7] - d[8])
        inv = 1.0 / density
        inner = pl.ds(ROW, cy)
        vel[0, i + 2, inner, :] = jx * inv
        vel[1, i + 2, inner, :] = jy * inv
        vel[2, i + 2, inner, :] = jz * inv
        return carry

    for i in range(nchunk):
        fetch(i).wait()
        lax.fori_loop(i * step, (i + 1) * step, moments_plane, 0)

    pl.semaphore_wait(barrier, greeted)

    def span_of(d, size, width):
        first = size[0]
        if d == 0:
            return pl.ds(first, size[1]), pl.ds(first, size[1])
        if d > 0:
            return pl.ds(first + size[1] - width, width), pl.ds(first - width, width)
        return pl.ds(first, width), pl.ds(first + size[1], width)

    def vel_copy(i):
        dz, dy = sides[i]
        zs, zt = span_of(dz, (2, cz), 2)
        ys, yt = span_of(dy, (ROW, cy), 2)
        return pltpu.make_async_remote_copy(
            src_ref=vel.at[:, zs, ys, :],
            dst_ref=vel.at[:, zt, yt, :],
            send_sem=v_send.at[i],
            recv_sem=v_recv.at[i],
            device_id=near(dz, dy),
            device_id_type=MESH,
        )

    for i in range(len(sides)):
        vel_copy(i).start()

    nmark, kk = cell_ref.shape
    nrows = cz * cy
    row_iota = lax.broadcasted_iota(jnp.int32, (nmark, nrows), 1)
    lane_iota = lax.broadcasted_iota(jnp.int32, (nmark, cx), 1)
    cells = cell_ref[...]
    weights = weight_ref[...]
    for k in range(kk):
        cell = cells[:, k : k + 1]
        line = cell // cx
        pick[k * nmark : (k + 1) * nmark, :] = jnp.where(row_iota == line, 1.0, 0.0).astype(
            jnp.bfloat16
        )
        lanes[k * nmark : (k + 1) * nmark, :] = jnp.where(
            lane_iota == cell - line * cx, weights[:, k : k + 1], 0.0
        )

    for i in range(len(sides)):
        vel_copy(i).wait_recv()

    def first_pass(i, carry):
        mid, low, high = pl.ds(ROW - 1, 40), pl.ds(ROW - 2, 40), pl.ds(ROW, 40)
        v = [vel[a, i + 1, mid, :] for a in range(3)]
        d = []
        for a in range(3):
            dx = roll_x(v[a], -1) - roll_x(v[a], 1)
            dy = vel[a, i + 1, high, :] - vel[a, i + 1, low, :]
            dz = vel[a, i + 2, mid, :] - vel[a, i, mid, :]
            d.append((dx, dy, dz))
        e, mag = strain_of(d)
        mags[i] = mag
        half_mag = 0.5 * mag
        for n in range(3):
            tmp[n] = smooth_x(mag * e[n])
            tmp[n + 3] = smooth_x(half_mag * e[n + 3])
        for n, (a, b) in enumerate(PAIRS):
            tmp[n + 6] = smooth_x(v[a] * v[b])
        for n in range(12):
            filt[n, i] = tri(tmp[n, 0:cy, :], tmp[n, 1 : cy + 1, :], tmp[n, 2 : cy + 2, :])
        for a in range(3):
            along_z = tri(vel[a, i, low, :], vel[a, i + 1, low, :], vel[a, i + 2, low, :])
            vtmp[a, 0:40, :] = smooth_x(along_z)
        for a in range(3):
            vhat[a, i] = (1.0 / 64.0) * tri(vtmp[a, 0:40, :], vtmp[a, 1:41, :], vtmp[a, 2:42, :])
        return carry

    lax.fori_loop(0, cz + 2, first_pass, 0)

    def second_pass(i, carry):
        plane_lm, plane_mm = carry
        mid, low, high = pl.ds(1, cy), pl.ds(0, cy), pl.ds(2, cy)
        v = [vhat[a, i + 1, mid, :] for a in range(3)]
        d = []
        for a in range(3):
            dx = roll_x(v[a], -1) - roll_x(v[a], 1)
            dy = vhat[a, i + 1, high, :] - vhat[a, i + 1, low, :]
            dz = vhat[a, i + 2, mid, :] - vhat[a, i, mid, :]
            d.append((dx, dy, dz))
        e, mag = strain_of(d)
        four, two = 4.0 * mag, 2.0 * mag
        lm = mm = lm_off = mm_off = None
        for n, (a, b) in enumerate(PAIRS):
            hat_ss = tri(filt[n, i], filt[n, i + 1], filt[n, i + 2])
            hat_vv = tri(filt[n + 6, i], filt[n + 6, i + 1], filt[n + 6, i + 2])
            model = (1.0 / 64.0) * hat_ss - (four if n < 3 else two) * e[n]
            leonard = (1.0 / 64.0) * hat_vv - v[a] * v[b]
            if n == 0:
                lm, mm = leonard * model, model * model
            elif n < 3:
                lm, mm = lm + leonard * model, mm + model * model
            elif n == 3:
                lm_off, mm_off = leonard * model, model * model
            else:
                lm_off, mm_off = lm_off + leonard * model, mm_off + model * model
        return plane_lm + (lm + 2.0 * lm_off), plane_mm + (mm + 2.0 * mm_off)

    zero = jnp.zeros((cy, cx), jnp.float32)
    plane_lm, plane_mm = lax.fori_loop(0, cz, second_pass, (zero, zero))

    rows = cy // nxc
    sums[0] = plane_lm
    sums[1] = plane_mm
    for j in range(nxc):
        d1s[j, 0:rows, :] = sums[0, j * rows : (j + 1) * rows, :]
        d1s[j, rows : 2 * rows, :] = sums[1, j * rows : (j + 1) * rows, :]

    def exchange(src, dst, slot, send, recv, dev, j):
        return pltpu.make_async_remote_copy(
            src_ref=src,
            dst_ref=dst.at[slot],
            send_sem=send.at[j],
            recv_sem=recv.at[slot],
            device_id=dev(j),
            device_id_type=MESH,
        )

    def for_others(me, count, act):
        def body(k, carry):
            act((me + k) % count)
            return carry

        lax.fori_loop(1, count, body, 0)

    def d1_send_to(j):
        exchange(d1s.at[j], d1r, xc, d1_send, d1_recv, xc_dev, j).start()

    def d1_from(j):
        exchange(d1s.at[j], d1r, j, d1_send, d1_recv, xc_dev, j).wait_recv()

    def d2_send_to(j):
        exchange(d2.at[z], d2, z, d2_send, d2_recv, z_dev, j).start()

    def d2_from(j):
        exchange(d2.at[z], d2, j, d2_send, d2_recv, z_dev, j).wait_recv()

    def d3_send_to(j):
        exchange(d3.at[xc], d3, xc, d3_send, d3_recv, xc_dev, j).start()

    def d3_from(j):
        exchange(d3.at[xc], d3, j, d3_send, d3_recv, xc_dev, j).wait_recv()

    def collide_plane(i, carry):
        inner = pl.ds(ROW, cy)
        f = [pops[q, i].astype(jnp.float32) for q in range(19)]
        sm, d = add_pairs(f)
        sx, sy, sz, sa, sb, sc, sd, se, sg = sm
        dx, dy, dz, da, db, dc, dd, de, dg = d
        ux, uy, uz = [vel[a, i + 2, inner, :] for a in range(3)]
        xy, xz, yz = sa + sb, sc + sd, se + sg
        axis, diag = sx + sy + sz, xy + xz + yz
        abp, abm, cdp, cdm, egp, egm = da + db, da - db, dc + dd, dc - dd, de + dg, de - dg
        jx, jy, jz = dx + (abp + cdp), dy + (abm + egp), dz + (cdm + egm)
        jxx, jyy, jzz = jx * ux, jy * uy, jz * uz
        ju = jxx + jyy + jzz
        ne = (1.19 * 19.0 / 2394.0) * (diag - f[0] - ju)
        neps = (1.4 / 252.0) * (9.0 * f[0] - 7.0 * axis - 2.0 * diag + 5.5 * ju)
        ax_part = -11.0 * ne - 4.0 * neps
        dg_part = 8.0 * ne + neps
        eq_xx = 3.0 * jxx - ju
        eq_ww = jyy - jzz
        axis_xx, diag_xx = 3.0 * sx - axis, diag - 3.0 * yz
        axis_ww, diag_ww = sy - sz, xy - xz
        pi_xx = (1.4 / 72.0) * (diag_xx - 2.0 * axis_xx + 0.5 * eq_xx)
        pi_ww = (1.4 / 24.0) * (diag_ww - 2.0 * axis_ww + 0.5 * eq_ww)
        shear[0, i] = (1.0 / 36.0) * (axis_xx + diag_xx - eq_xx)
        shear[1, i] = (1.0 / 12.0) * (axis_ww + diag_ww - eq_ww)
        shear[2, i] = 0.25 * (sa - sb - jx * uy)
        shear[3, i] = 0.25 * (sc - sd - jx * uz)
        shear[4, i] = 0.25 * (se - sg - jy * uz)
        two_xx, two_ww = 2.0 * pi_xx, 2.0 * pi_ww
        base_yz = ax_part + two_xx
        hx = ax_part - 2.0 * two_xx
        hy, hz = base_yz - two_ww, base_yz + two_ww
        base_d = dg_part + pi_xx
        hxy, hxz, hyz = base_d + pi_ww, base_d - pi_ww, dg_part - two_xx
        tx = (1.2 / 8.0) * ((1.0 / 3.0) * jx - dx)
        ty = (1.2 / 8.0) * ((1.0 / 3.0) * jy - dy)
        tz = (1.2 / 8.0) * ((1.0 / 3.0) * jz - dz)
        mx = (1.98 / 8.0) * (abp - cdp)
        my = (1.98 / 8.0) * (egp - abm)
        mz = (1.98 / 8.0) * (cdm - egm)
        xp, xm, yp, ym, zp, zm = tx + mx, tx - mx, ty + my, ty - my, tz + mz, tz - mz
        halves = [
            (hx, -4.0 * tx),
            (hy, -4.0 * ty),
            (hz, -4.0 * tz),
            (hxy, xp + ym),
            (hxy, xp - ym),
            (hxz, xm + zp),
            (hxz, xm - zp),
            (hyz, yp + zm),
            (hyz, yp - zm),
        ]
        part[0, i] = f[0] + (30.0 * ne - 12.0 * neps)
        for n, (even, odd) in enumerate(halves):
            part[2 * n + 1, i] = f[2 * n + 1] - (even + odd)
            part[2 * n + 2, i] = f[2 * n + 2] - (even - odd)
        return carry

    third = (cz + 2) // 3

    for_others(xc, nxc, d1_send_to)
    d1r[xc] = d1s[xc]
    lax.fori_loop(0, third, collide_plane, 0)
    for_others(xc, nxc, d1_from)
    total = d1r[0]
    for j in range(1, nxc):
        total = total + d1r[j]
    d2[z] = total
    for_others(z, nz, d2_send_to)
    lax.fori_loop(third, 2 * third, collide_plane, 0)
    for_others(z, nz, d2_from)
    total = d2[0]
    for j in range(1, nz):
        total = total + d2[j]
    d1r[0] = total
    eddy_rows = jnp.maximum(d1r[0, 0:rows, :] / (d1r[0, rows : 2 * rows, :] + eps_sum), 0.0)
    d3[xc, 0:rows, :] = eddy_rows
    d3[xc, rows : 2 * rows, :] = eddy_rows
    for_others(xc, nxc, d3_send_to)
    lax.fori_loop(2 * third, cz, collide_plane, 0)
    for_others(xc, nxc, d3_from)
    for j in range(nxc):
        eddy_ref[j * rows : (j + 1) * rows, :] = d3[j, 0:rows, :]

    def finish_plane(i, carry):
        mag = mags[i + 1, 1 : cy + 1, :]
        rate = 1.0 / (0.5 + 3.0 * (base_visc + eddy_ref[...] * mag))
        rxx, rww, rxy, rxz, ryz = [rate * shear[n, i] for n in range(5)]
        diag_y, diag_z, diag_yz = rxx + rww, rxx - rww, -2.0 * rxx
        lost = [
            2.0 * rxx,
            rww - rxx,
            -diag_y,
            diag_y + rxy,
            diag_y - rxy,
            diag_z + rxz,
            diag_z - rxz,
            diag_yz + ryz,
            diag_yz - ryz,
        ]
        inner = pl.ds(ROW, cy)

        def keep(q, value):
            post[PLACE[q], i + 1, inner, :] = value.astype(jnp.bfloat16).astype(jnp.float32)

        keep(0, part[0, i])
        for n in range(9):
            keep(2 * n + 1, part[2 * n + 1, i] - lost[n])
            keep(2 * n + 2, part[2 * n + 2, i] - lost[n])
        return carry

    lax.fori_loop(0, cz, finish_plane, 0)

    crossing = [
        ((1, 0), 0, 5),
        ((-1, 0), 8, 5),
        ((0, 1), 4, 5),
        ((0, -1), 12, 4),
        ((0, -1), 0, 1),
        ((1, 1), 4, 1),
        ((1, -1), 0, 1),
        ((-1, 1), 8, 1),
        ((-1, -1), 12, 1),
    ]

    def post_copy(i):
        (dz, dy), first, count = crossing[i]
        zs, zt = span_of(dz, (1, cz), 1)
        ys, yt = span_of(dy, (ROW, cy), 1)
        group = pl.ds(first, count)
        return pltpu.make_async_remote_copy(
            src_ref=post.at[group, zs, ys, :],
            dst_ref=post.at[group, zt, yt, :],
            send_sem=p_send.at[i],
            recv_sem=p_recv.at[i],
            device_id=near(dz, dy),
            device_id_type=MESH,
        )

    for i in range(len(crossing)):
        post_copy(i).start()
    for i in range(len(crossing)):
        post_copy(i).wait_recv()

    def put(i):
        return pltpu.make_async_copy(outv.at[:, i], out_hbm.at[:, i], out_sem.at[i])

    def stream_plane(i, carry):
        f = []
        for q, (ex, ey, ez) in enumerate(VELOCITIES):
            value = post[PLACE[q], i + 1 - ez, pl.ds(ROW - ey, cy), :]
            if ex:
                value = roll_x(value, ex)
            outv[q, i] = value.astype(jnp.bfloat16)
            f.append(value)
        put(i).start()
        d = [f[2 * n + 1] - f[2 * n + 2] for n in range(9)]
        jx = d[0] + (d[3] + d[4]) + (d[5] + d[6])
        jy = d[1] + (d[3] - d[4]) + (d[7] + d[8])
        jz = d[2] + (d[5] - d[6]) + (d[7] - d[8])
        lines = pl.ds(pl.multiple_of(i * cy, cy), cy)
        for n, value in enumerate((jx, jy, jz)):
            high = value.astype(jnp.bfloat16)
            low = (value - high.astype(jnp.float32)).astype(jnp.bfloat16)
            mom[lines, 2 * n * cx : (2 * n + 1) * cx] = high
            mom[lines, (2 * n + 1) * cx : (2 * n + 2) * cx] = low
        return carry

    lax.fori_loop(0, cz, stream_plane, 0)

    gath[...] = jnp.dot(pick[...], mom[...], preferred_element_type=jnp.float32)
    forces = []
    ones = jnp.ones((8, cx), jnp.bfloat16)

    def parts_of(value):
        first = value.astype(jnp.bfloat16)
        rest = value - first.astype(jnp.float32)
        second = rest.astype(jnp.bfloat16)
        third_part = (rest - second.astype(jnp.float32)).astype(jnp.bfloat16)
        return first, second, third_part

    def dot_t(a, b):
        return lax.dot_general(a, b, (((1,), (1,)), ((), ())), preferred_element_type=jnp.float32)

    for n in range(3):
        acc = None
        for k in range(kk):
            block = pl.ds(k * nmark, nmark)
            both = (
                gath[block, 2 * n * cx : (2 * n + 1) * cx]
                + gath[block, (2 * n + 1) * cx : (2 * n + 2) * cx]
            )
            term = lanes[block, :] * both
            acc = term if acc is None else acc + term
        a, b, e = parts_of(acc)
        forces.append(-(dot_t(ones, a) + dot_t(ones, b) + dot_t(ones, e)))
    which = lax.broadcasted_iota(jnp.int32, (8, nmark), 0)
    force = jnp.where(which == 0, forces[0], jnp.where(which == 1, forces[1], forces[2]))
    a, b, e = parts_of(force)
    ids = seg_ref[...].reshape(1, nmark)
    lane_count = SEG_DEV * ng2
    seg_iota = lax.broadcasted_iota(jnp.int32, (lane_count, nmark), 0)
    for j in range(ng1):
        hot = jnp.where(seg_iota == ids - j * lane_count, 1.0, 0.0).astype(jnp.bfloat16)
        h1s[j] = dot_t(a, hot) + dot_t(b, hot) + dot_t(e, hot)

    def h1_send_to(j):
        exchange(h1s.at[j], h1r, g1, h1_send, h1_recv, g1_dev, j).start()

    def h1_from(j):
        exchange(h1s.at[j], h1r, j, h1_send, h1_recv, g1_dev, j).wait_recv()

    def h2_send_to(j):
        exchange(h2.at[g2], h2, g2, h2_send, h2_recv, g2_dev, j).start()

    def h2_from(j):
        exchange(h2.at[g2], h2, j, h2_send, h2_recv, g2_dev, j).wait_recv()

    for_others(g1, ng1, h1_send_to)
    h1r[g1] = h1s[g1]
    for_others(g1, ng1, h1_from)
    total = h1r[0]
    for j in range(1, ng1):
        total = total + h1r[j]
    h2[g2] = total
    for_others(g2, ng2, h2_send_to)
    for_others(g2, ng2, h2_from)
    total = h2[0]
    for j in range(1, ng2):
        total = total + h2[j]
    mine = pltpu.roll(total, (lane_count - g2 * SEG_DEV) % lane_count, axis=1)
    force_ref[...] = mine[0:3, 0:SEG_DEV]

    for i in range(len(sides)):
        vel_copy(i).wait_send()
    for i in range(len(crossing)):
        post_copy(i).wait_send()

    def d1_sent(j):
        exchange(d1s.at[j], d1r, xc, d1_send, d1_recv, xc_dev, j).wait_send()

    def d2_sent(j):
        exchange(d2.at[z], d2, z, d2_send, d2_recv, z_dev, j).wait_send()

    def d3_sent(j):
        exchange(d3.at[xc], d3, xc, d3_send, d3_recv, xc_dev, j).wait_send()

    def h1_sent(j):
        exchange(h1s.at[j], h1r, g1, h1_send, h1_recv, g1_dev, j).wait_send()

    def h2_sent(j):
        exchange(h2.at[g2], h2, g2, h2_send, h2_recv, g2_dev, j).wait_send()

    for_others(xc, nxc, d1_sent)
    for_others(z, nz, d2_sent)
    for_others(xc, nxc, d3_sent)
    for_others(g1, ng1, h1_sent)
    for_others(g2, ng2, h2_sent)

    def put_done(i, carry):
        put(i).wait()
        return carry

    lax.fori_loop(0, cz, put_done, 0)


def local(split, populations, cell_index, marker_weight, segment_id):
    nq, cz, cy, cx = populations.shape
    nmark, kk = cell_index.shape
    nz, nx, nc, ny = split
    nxc = nx * nc
    ng1, ng2 = nz * (nx // 2), 2 * nc * ny
    rows = cy // nxc
    f32, bf16 = jnp.float32, jnp.bfloat16
    dma = pltpu.SemaphoreType.DMA
    vmem = pl.BlockSpec(memory_space=pltpu.VMEM)
    hbm = pl.BlockSpec(memory_space=pl.ANY)
    lane_count = SEG_DEV * ng2
    scratch = [
        pltpu.VMEM((nq, cz, cy, cx), bf16),
        pltpu.VMEM((3, cz + 4, TOP, cx), f32),
        pltpu.VMEM((cz + 2, 40, cx), f32),
        pltpu.VMEM((12, 40, cx), f32),
        pltpu.VMEM((3, 48, cx), f32),
        pltpu.VMEM((3, cz + 2, 40, cx), f32),
        pltpu.VMEM((12, cz + 2, cy, cx), f32),
        pltpu.VMEM((2, cy, cx), f32),
        pltpu.VMEM((nq, cz, cy, cx), f32),
        pltpu.VMEM((5, cz, cy, cx), f32),
        pltpu.VMEM((nq, cz + 2, TOP, cx), f32),
        pltpu.VMEM((nq, cz, cy, cx), bf16),
        pltpu.VMEM((cz * cy, 6 * cx), bf16),
        pltpu.VMEM((kk * nmark, cz * cy), bf16),
        pltpu.VMEM((kk * nmark, cx), f32),
        pltpu.VMEM((kk * nmark, 6 * cx), f32),
        pltpu.VMEM((nxc, 2 * rows, cx), f32),
        pltpu.VMEM((nxc, 2 * rows, cx), f32),
        pltpu.VMEM((nz, 2 * rows, cx), f32),
        pltpu.VMEM((nxc, 2 * rows, cx), f32),
        pltpu.VMEM((ng1, 8, lane_count), f32),
        pltpu.VMEM((ng1, 8, lane_count), f32),
        pltpu.VMEM((ng2, 8, lane_count), f32),
        dma((4,)),
        dma((cz,)),
        dma((8,)),
        dma((8,)),
        dma((9,)),
        dma((9,)),
        dma((nxc,)),
        dma((nxc,)),
        dma((nz,)),
        dma((nz,)),
        dma((nxc,)),
        dma((nxc,)),
        dma((ng1,)),
        dma((ng1,)),
        dma((ng2,)),
        dma((ng2,)),
    ]
    return pl.pallas_call(
        functools.partial(kernel, split),
        out_shape=(
            jax.ShapeDtypeStruct((nq, cz, cy, cx), bf16),
            jax.ShapeDtypeStruct((cy, cx), f32),
            jax.ShapeDtypeStruct((3, SEG_DEV), f32),
        ),
        in_specs=[hbm, vmem, vmem, vmem],
        out_specs=(hbm, vmem, vmem),
        scratch_shapes=scratch,
        compiler_params=pltpu.CompilerParams(
            collective_id=0, has_side_effects=True, vmem_limit_bytes=50 * 1024 * 1024
        ),
    )(populations, cell_index, marker_weight, segment_id)


def solution(mesh):
    in_specs = (
        P(None, "span", "cross", None),
        P(("span", "cross"), None),
        P(("span", "cross"), None),
        P(("span", "cross")),
    )
    out_specs = (P(None, "span", "cross", None), P("cross", None), P(None, ("span", "cross")))
    sizes = dict(mesh.shape)
    split = (sizes["span"] // (CHIPS_X * CORES), CHIPS_X, CORES, sizes["cross"])
    return jax.shard_map(
        functools.partial(local, split),
        mesh=mesh,
        in_specs=in_specs,
        out_specs=out_specs,
        check_vma=False,
    )
```

time: 467 us -> 66.4 us (0.14); the launches traced: 458 us -> 66.2 us
  blocking collectives: 337 us -> 0 us
  Pallas kernels: 0 us -> 60.7 us
  local copies, waits for them, and re-layouts: 54.4 us -> 4.86 us
  matrix products: 25.1 us -> 0 us
  other arithmetic: 19.5 us -> 0 us
  starting transfers between devices: 14.7 us -> 0 us
  waiting for transfers between devices: 5.54 us -> 0 us
    psum x1 -> x0, blocking collectives: 248 us -> none  [local(): total_lm, total_mm = lax.psum((plane_lm, plane_mm), 'span')]
    unnamed x1 -> x0, blocking collectives: 88.5 us -> none
    pallas_call x0 -> x1, Pallas kernels: none -> 60.7 us  [local(): pl.pallas_call(functools.partial(kernel, split), out_shape=(jax.ShapeDtyp...]
    dot_general x4 -> x0, matrix products: 25.1 us -> none  [the longest x1 8.68 us: collide(): jnp.dot(jnp.asarray(velocities, jnp.float32), velocity, precision=lax.Pre...]
    dot_general x1 -> x0, local copies, waits for them, and re-layouts: 15.9 us -> none  [local(): jnp.dot(jnp.asarray(moment_basis()[1:], jnp.bfloat16), populations_next.r...]
    ppermute x8 -> x0, starting transfers between devices: 14.7 us -> none  [the longest x4 9.8 us: extended(): lax.ppermute(lax.slice_in_dim(block, 0, width, axis=dim), axis, backward)]
    gather x1 -> x0, local copies, waits for them, and re-layouts: 13.4 us -> none  [local(): picked = momentum[:, cell_index]]
    unnamed x84 -> x7, local copies, waits for them, and re-layouts: 15.5 us -> 4.86 us
  transfers between devices with their start and end apart: 8 -> 0, of which waited for: 4 -> 0; matrix products, arithmetic and copies ran while one was open for 3% -> 0% of each run, Pallas kernels for 0% -> 0%
where the time goes in v1:
time: 66.4 us; the launch traced here: 66.2 us
  Pallas kernels  60.7 us (91%)
  local copies, waits for them, and re-layouts  4.86 us (7%)
    pallas_call x1, Pallas kernels, local(): pl.pallas_call(functools.partial(kernel, split), out_shape=(jax.ShapeDtyp...  60.7 us
    unnamed x7, local copies, waits for them, and re-layouts  4.86 us

profile of v1, /device:TPU:1, one launch (start us, length us, event | category | flops | bytes accessed | tf_op | source)
XLA Modules:
  0.0 66.2 jit_solution(14233973822802800002)
XLA Ops:
  0.6 0.8 %copy.7.cell_ref = s32[128,8]{1,0:T(8,128)S(1)} copy(s32[128,8]{0,1:T(8,128)} %param.5) | data formatting | bytes 8192 | tf_op args[1]
  1.4 0.8 %copy.8.weight_ref = f32[128,8]{1,0:T(8,128)S(1)} copy(f32[128,8]{0,1:T(8,128)} %param.6) | data formatting | bytes 8192 | tf_op args[2]
  2.2 0.0 copy-start
  2.2 0.6 copy-done
  2.9 60.7 %shard_map.67 = (bf16[19,16,32,128]{3,2,1,0:T(8,128)(2,1)S(1)}, f32[32,128]{1,0:T(8,128)S(1)}, f32[3,8]{1,0:T(4,128)S(1)}) custom-call(bf16[19,16,32,128]{3,2,1,0:T(8,128)(2,1)} %pops_hbm.1, s32[128,8]{1,0:T(8,128)S(1)} %copy.7.cell_ref, f32[128,8]{1,0:T(8,128)S(1)} %copy.8.weight_ref, s32[128]{0:T(128)S(1)} %copy-done), custom_call_target="tpu_custom_call" | custom-call | tf_op jit(solution)/shard_map/pallas_call | solution.py:670
  63.6 1.5 %copy.12 = bf16[19,16,32,128]{3,2,1,0:T(8,128)(2,1)} copy(bf16[19,16,32,128]{3,2,1,0:T(8,128)(2,1)S(1)} %get-tuple-element.6) | data formatting | bytes 4980736
  65.1 0.6 copy.13
  65.7 0.6 copy.14
Async XLA Ops:
  2.2 0.7 copy-start

commit v2 on v1

v2 whole, which is shorter than its diff:
```python
import functools

import jax
import jax.numpy as jnp
from jax import lax
from jax.experimental import pallas as pl
from jax.experimental.pallas import tpu as pltpu
from jax.sharding import PartitionSpec as P

SEG_DEV = 8
MESH = pl.DeviceIdType.MESH
eps_sum = 1e-06
base_visc = 0.005

CHIPS_X = 4
CORES = 2

VELOCITIES = [
    (0, 0, 0),
    (1, 0, 0),
    (-1, 0, 0),
    (0, 1, 0),
    (0, -1, 0),
    (0, 0, 1),
    (0, 0, -1),
    (1, 1, 0),
    (-1, -1, 0),
    (1, -1, 0),
    (-1, 1, 0),
    (1, 0, 1),
    (-1, 0, -1),
    (1, 0, -1),
    (-1, 0, 1),
    (0, 1, 1),
    (0, -1, -1),
    (0, 1, -1),
    (0, -1, 1),
]
ORDER = [18, 5, 11, 14, 15, 3, 7, 10, 17, 6, 12, 13, 16, 4, 8, 9, 0, 1, 2]
PLACE = [ORDER.index(q) for q in range(19)]

ROW = 8
TOP = 48


def add_pairs(f):
    s = [f[2 * i + 1] + f[2 * i + 2] for i in range(9)]
    d = [f[2 * i + 1] - f[2 * i + 2] for i in range(9)]
    return s, d


def tri(low, mid, high):
    return (low + high) + (mid + mid)


def roll_x(a, shift):
    return pltpu.roll(a, shift % a.shape[-1], axis=a.ndim - 1)


def strain_of(d):
    exy, exz, eyz = d[0][1] + d[1][0], d[0][2] + d[2][0], d[1][2] + d[2][1]
    diag = d[0][0] * d[0][0] + d[1][1] * d[1][1] + d[2][2] * d[2][2]
    off = exy * exy + exz * exz + eyz * eyz
    mag = jnp.sqrt(0.5 * diag + 0.25 * off)
    return (d[0][0], d[1][1], d[2][2], exy, exz, eyz), mag


PAIRS = [(0, 0), (1, 1), (2, 2), (0, 1), (0, 2), (1, 2)]


SIDES = [(1, 0), (-1, 0), (0, 1), (0, -1), (1, 1), (1, -1), (-1, 1), (-1, -1)]
XZ, XX, WW, YZ, XY = range(5)


def near(split, dz, dy):
    nz, nx, nc, ny = split
    nspan = nz * nx * nc
    s, y = lax.axis_index("span"), lax.axis_index("cross")
    return ((s + dz + nspan) % nspan, (y + dy + ny) % ny)


def ranges(d, first, size, width):
    if d == 0:
        return pl.ds(first, size), pl.ds(first, size)
    if d > 0:
        return pl.ds(first + size - width, width), pl.ds(first - width, width)
    return pl.ds(first, width), pl.ds(first + size, width)


def velocity_kernel(split, pops_hbm, vel, pops, in_sem, v_send, v_recv):
    cz, cy, cx = pops.shape[1:]
    nchunk = in_sem.shape[0]
    step = cz // nchunk

    def fetch(i):
        some = pl.ds(i * step, step)
        return pltpu.make_async_copy(pops_hbm.at[:, some], pops.at[:, some], in_sem.at[i])

    for i in range(nchunk):
        fetch(i).start()
    barrier = pltpu.get_barrier_semaphore()
    for dz, dy in SIDES:
        pl.semaphore_signal(
            barrier, inc=1, device_id=near(split, dz, dy), device_id_type=MESH
        )

    def moments_plane(i, carry):
        f = [pops[q, i].astype(jnp.float32) for q in range(19)]
        sm, d = add_pairs(f)
        density = f[0] + ((sm[0] + sm[1] + sm[2]) + (sm[3] + sm[4] + sm[5]) + (sm[6] + sm[7] + sm[8]))
        jx = d[0] + (d[3] + d[4]) + (d[5] + d[6])
        jy = d[1] + (d[3] - d[4]) + (d[7] + d[8])
        jz = d[2] + (d[5] - d[6]) + (d[7] - d[8])
        inv = 1.0 / density
        inner = pl.ds(ROW, cy)
        vel[0, i + 2, inner, :] = jx * inv
        vel[1, i + 2, inner, :] = jy * inv
        vel[2, i + 2, inner, :] = jz * inv
        return carry

    for i in range(nchunk):
        fetch(i).wait()
        lax.fori_loop(i * step, (i + 1) * step, moments_plane, 0)

    pl.semaphore_wait(barrier, len(SIDES))

    def vel_copy(i):
        dz, dy = SIDES[i]
        zs, zt = ranges(dz, 2, cz, 2)
        ys, yt = ranges(dy, ROW, cy, 2)
        return pltpu.make_async_remote_copy(
            src_ref=vel.at[:, zs, ys, :],
            dst_ref=vel.at[:, zt, yt, :],
            send_sem=v_send.at[i],
            recv_sem=v_recv.at[i],
            device_id=near(split, dz, dy),
            device_id_type=MESH,
        )

    for i in range(len(SIDES)):
        vel_copy(i).start()
    for i in range(len(SIDES)):
        vel_copy(i).wait()


def step_kernel(
    split,
    vel,
    pops,
    cell_ref,
    weight_ref,
    seg_ref,
    outv,
    eddy_ref,
    force_ref,
    smoother,
    hats_a,
    hats_b,
    mags,
    tmp_a,
    tmp_b,
    vtmp_a,
    vtmp_b,
    vhat,
    filt,
    sums,
    shear,
    post,
    eddyx,
    mom,
    pick,
    lanes,
    gath,
    hot,
    d1s,
    d1r,
    d2,
    d3,
    dlow,
    dhigh,
    h1s,
    h1r,
    h2,
    p_send,
    p_recv,
    s_send,
    s_recv,
    d1_send,
    d1_recv,
    d2_send,
    d2_recv,
    d3_send,
    d3_recv,
    e_send,
    e_recv,
    h1_send,
    h1_recv,
    h2_send,
    h2_recv,
):
    nz, nx, nc, ny = split
    nxc = nx * nc
    cz, cy, cx = pops.shape[1:]
    half = nx // 2
    ng1, ng2 = nz * half, 2 * nc * ny
    s = lax.axis_index("span")
    y = lax.axis_index("cross")
    z, xc = s // nxc, s % nxc
    x, c = xc // nc, xc % nc
    g1 = z * half + x // 2
    g2 = y * (2 * nc) + (x % 2) * nc + c
    place = (x % 2) * (nc * ny) + c * ny + y
    y_up, y_down = (y + 1) % ny, (y + ny - 1) % ny

    def xc_dev(j):
        return (z * nxc + j, y)

    def z_dev(j):
        return (j * nxc + xc, y)

    def g1_dev(j):
        return ((j // half) * nxc + ((j % half) * 2 + x % 2) * nc + c, y)

    def g2_dev(j):
        return (z * nxc + (x // 2) * (2 * nc) + j % (2 * nc), j // (2 * nc))

    def for_others(me, count, act, unroll=False):
        def body(t, carry):
            away = count // 2 + (t // 2) * (1 - 2 * (t % 2))
            act((me + away) % count)
            return carry

        lax.fori_loop(1, count, body, 0, unroll=unroll)

    def for_all(count, act):
        def body(j, carry):
            act(j)
            return carry

        lax.fori_loop(0, count, body, 0)

    barrier = pltpu.get_barrier_semaphore()

    def greet(dev):
        pl.semaphore_signal(barrier, inc=1, device_id=dev, device_id_type=MESH)

    for_others(g1, ng1, lambda j: greet(g1_dev(j)))
    for_others(g2, ng2, lambda j: greet(g2_dev(j)))
    for_others(z, nz, lambda j: greet(z_dev(j)))
    for_others(xc, nxc, lambda j: greet(xc_dev(j)))
    for dz, dy in SIDES:
        greet(near(split, dz, dy))
    greet((z * nxc + nxc - 1, y_down))
    greet((z * nxc, y_up))
    last, first = xc == nxc - 1, xc == 0
    greeted = len(SIDES) + (nxc - 1) + (nz - 1) + (ng1 - 1) + (ng2 - 1)
    greeted = greeted + jnp.where(jnp.logical_or(last, first), nxc, 0)

    apart = lax.broadcasted_iota(jnp.int32, (cx, cx), 0) - lax.broadcasted_iota(jnp.int32, (cx, cx), 1)
    apart = (apart + cx) % cx
    beside = jnp.logical_or(apart == 1, apart == cx - 1)
    circulant = jnp.where(apart == 0, 2.0, jnp.where(beside, 1.0, 0.0)).astype(jnp.bfloat16)
    for n in range(3):
        smoother[n * cx : (n + 1) * cx, :] = circulant

    def smooth_x(values):
        both = jnp.concatenate(values, axis=0)
        high = both.astype(jnp.bfloat16)
        rest = both - high.astype(jnp.float32)
        mid = rest.astype(jnp.bfloat16)
        low = (rest - mid.astype(jnp.float32)).astype(jnp.bfloat16)
        parts = jnp.concatenate([high, mid, low], axis=1)
        return jnp.dot(parts, smoother[...], preferred_element_type=jnp.float32)

    def products(p, tmp, vtmp):
        mid, low, high = pl.ds(ROW - 1, 40), pl.ds(ROW - 2, 40), pl.ds(ROW, 40)
        v = [vel[a, p + 1, mid, :] for a in range(3)]
        for n, (a, b) in enumerate(PAIRS):
            tmp[n + 6] = v[a] * v[b]
        d = []
        for a in range(3):
            below = vel[a, p + 1, low, :]
            vtmp[a, 0:40, :] = tri(vel[a, p, low, :], below, vel[a, p + 2, low, :])
            dx = roll_x(v[a], -1) - roll_x(v[a], 1)
            dy = vel[a, p + 1, high, :] - below
            dz = vel[a, p + 2, mid, :] - vel[a, p, mid, :]
            d.append((dx, dy, dz))
        e, mag = strain_of(d)
        mags[p] = mag
        half_mag = 0.5 * mag
        for n in range(3):
            tmp[n] = mag * e[n]
            tmp[n + 3] = half_mag * e[n + 3]

    def filters(p, tmp, vtmp):
        for n in range(12):
            filt[n, p + 1] = tri(tmp[n, 0:cy, :], tmp[n, 1 : cy + 1, :], tmp[n, 2 : cy + 2, :])
        along_y = [tri(vtmp[a, 0:40, :], vtmp[a, 1:41, :], vtmp[a, 2:42, :]) for a in range(3)]
        smoothed = smooth_x(along_y)
        for a in range(3):
            vhat[a, p + 1] = (1.0 / 64.0) * smoothed[a * 40 : (a + 1) * 40]

    def two_planes(i, carry):
        products(2 * i, tmp_a, vtmp_a)
        filters(2 * i - 1, tmp_b, vtmp_b)
        products(2 * i + 1, tmp_b, vtmp_b)
        filters(2 * i, tmp_a, vtmp_a)
        return carry

    lax.fori_loop(0, (cz + 2) // 2, two_planes, 0)
    filters(cz + 1, tmp_b, vtmp_b)

    def hats_of(i, hats):
        along_z = [tri(filt[n, i + 1], filt[n, i + 2], filt[n, i + 3]) for n in range(12)]
        smoothed = smooth_x(along_z)
        for n in range(12):
            hats[n] = (1.0 / 64.0) * smoothed[n * cy : (n + 1) * cy]

    def add_plane(i, hats, plane_lm, plane_mm):
        mid, low, high = pl.ds(1, cy), pl.ds(0, cy), pl.ds(2, cy)
        v = [vhat[a, i + 2, mid, :] for a in range(3)]
        d = []
        for a in range(3):
            dx = roll_x(v[a], -1) - roll_x(v[a], 1)
            dy = vhat[a, i + 2, high, :] - vhat[a, i + 2, low, :]
            dz = vhat[a, i + 3, mid, :] - vhat[a, i + 1, mid, :]
            d.append((dx, dy, dz))
        e, mag = strain_of(d)
        four, two = 4.0 * mag, 2.0 * mag
        lm = mm = lm_off = mm_off = None
        for n, (a, b) in enumerate(PAIRS):
            model = hats[n] - (four if n < 3 else two) * e[n]
            leonard = hats[n + 6] - v[a] * v[b]
            if n == 0:
                lm, mm = leonard * model, model * model
            elif n < 3:
                lm, mm = lm + leonard * model, mm + model * model
            elif n == 3:
                lm_off, mm_off = leonard * model, model * model
            else:
                lm_off, mm_off = lm_off + leonard * model, mm_off + model * model
        return plane_lm + (lm + 2.0 * lm_off), plane_mm + (mm + 2.0 * mm_off)

    def second_pass(i, carry):
        hats_of(2 * i + 1, hats_b)
        carry = add_plane(2 * i, hats_a, *carry)
        hats_of(2 * i + 2, hats_a)
        return add_plane(2 * i + 1, hats_b, *carry)

    zero = jnp.zeros((cy, cx), jnp.float32)
    hats_of(0, hats_a)
    plane_lm, plane_mm = lax.fori_loop(0, cz // 2, second_pass, (zero, zero))

    rows = cy // nxc
    sums[0] = plane_lm
    sums[1] = plane_mm
    for j in range(nxc):
        d1s[j, 0:rows, :] = sums[0, j * rows : (j + 1) * rows, :]
        d1s[j, rows : 2 * rows, :] = sums[1, j * rows : (j + 1) * rows, :]

    def exchange(src, dst, slot, send, recv, dev, j):
        return pltpu.make_async_remote_copy(
            src_ref=src,
            dst_ref=dst.at[slot],
            send_sem=send.at[j],
            recv_sem=recv.at[slot],
            device_id=dev(j),
            device_id_type=MESH,
        )

    def d1_copy(j, slot):
        return exchange(d1s.at[j], d1r, slot, d1_send, d1_recv, xc_dev, j)

    def d2_copy(j, slot):
        return exchange(d2.at[z], d2, slot, d2_send, d2_recv, z_dev, j)

    def d3_copy(j, slot):
        return exchange(d3.at[xc], d3, slot, d3_send, d3_recv, xc_dev, j)

    def edge_copy(j, side):
        return pltpu.make_async_remote_copy(
            src_ref=d3.at[xc],
            dst_ref=dlow if side == 0 else dhigh,
            send_sem=e_send.at[side, j],
            recv_sem=e_recv.at[side],
            device_id=(z * nxc + j, y_up if side == 0 else y_down),
            device_id_type=MESH,
        )

    def h1_copy(j, slot):
        return exchange(h1s.at[j], h1r, slot, h1_send, h1_recv, g1_dev, j)

    def h2_copy(j, slot):
        return exchange(h2.at[g2], h2, slot, h2_send, h2_recv, g2_dev, j)

    pl.semaphore_wait(barrier, greeted)
    for_others(xc, nxc, lambda j: d1_copy(j, xc).start())

    inner = pl.ds(ROW, cy)

    def collide_plane(i, carry):
        f = [pops[q, i].astype(jnp.float32) for q in range(19)]
        sm, d = add_pairs(f)
        sx, sy, sz, sa, sb, sc, sd, se, sg = sm
        dx, dy, dz, da, db, dc, dd, de, dg = d
        ux, uy, uz = [vel[a, i + 2, inner, :] for a in range(3)]
        xy, xz, yz = sa + sb, sc + sd, se + sg
        axis, diag = sx + sy + sz, xy + xz + yz
        abp, abm, cdp, cdm, egp, egm = da + db, da - db, dc + dd, dc - dd, de + dg, de - dg
        jx, jy, jz = dx + (abp + cdp), dy + (abm + egp), dz + (cdm + egm)
        jxx, jyy, jzz = jx * ux, jy * uy, jz * uz
        ju = jxx + jyy + jzz
        ne = (1.19 * 19.0 / 2394.0) * (diag - f[0] - ju)
        neps = (1.4 / 252.0) * (9.0 * f[0] - 7.0 * axis - 2.0 * diag + 5.5 * ju)
        ax_part = -11.0 * ne - 4.0 * neps
        dg_part = 8.0 * ne + neps
        eq_xx = 3.0 * jxx - ju
        eq_ww = jyy - jzz
        axis_xx, diag_xx = 3.0 * sx - axis, diag - 3.0 * yz
        axis_ww, diag_ww = sy - sz, xy - xz
        pi_xx = (1.4 / 72.0) * (diag_xx - 2.0 * axis_xx + 0.5 * eq_xx)
        pi_ww = (1.4 / 24.0) * (diag_ww - 2.0 * axis_ww + 0.5 * eq_ww)
        shear[XX, i + 1, inner, :] = (1.0 / 36.0) * (axis_xx + diag_xx - eq_xx)
        shear[WW, i + 1, inner, :] = (1.0 / 12.0) * (axis_ww + diag_ww - eq_ww)
        shear[XY, i + 1, inner, :] = 0.25 * (sa - sb - jx * uy)
        shear[XZ, i + 1, inner, :] = 0.25 * (sc - sd - jx * uz)
        shear[YZ, i + 1, inner, :] = 0.25 * (se - sg - jy * uz)
        two_xx, two_ww = 2.0 * pi_xx, 2.0 * pi_ww
        base_yz = ax_part + two_xx
        hx = ax_part - 2.0 * two_xx
        hy, hz = base_yz - two_ww, base_yz + two_ww
        base_d = dg_part + pi_xx
        hxy, hxz, hyz = base_d + pi_ww, base_d - pi_ww, dg_part - two_xx
        tx = (1.2 / 8.0) * ((1.0 / 3.0) * jx - dx)
        ty = (1.2 / 8.0) * ((1.0 / 3.0) * jy - dy)
        tz = (1.2 / 8.0) * ((1.0 / 3.0) * jz - dz)
        mx = (1.98 / 8.0) * (abp - cdp)
        my = (1.98 / 8.0) * (egp - abm)
        mz = (1.98 / 8.0) * (cdm - egm)
        xp, xm, yp, ym, zp, zm = tx + mx, tx - mx, ty + my, ty - my, tz + mz, tz - mz
        halves = [
            (hx, -4.0 * tx),
            (hy, -4.0 * ty),
            (hz, -4.0 * tz),
            (hxy, xp + ym),
            (hxy, xp - ym),
            (hxz, xm + zp),
            (hxz, xm - zp),
            (hyz, yp + zm),
            (hyz, yp - zm),
        ]
        post[PLACE[0], i + 1, inner, :] = f[0] + (30.0 * ne - 12.0 * neps)
        for n, (even, odd) in enumerate(halves):
            post[PLACE[2 * n + 1], i + 1, inner, :] = f[2 * n + 1] - (even + odd)
            post[PLACE[2 * n + 2], i + 1, inner, :] = f[2 * n + 2] - (even - odd)
        return carry

    lax.fori_loop(0, cz, collide_plane, 0)

    crossing = [
        ((1, 0), 0, 5),
        ((-1, 0), 8, 5),
        ((0, 1), 4, 5),
        ((0, -1), 12, 4),
        ((0, -1), 0, 1),
        ((1, 1), 4, 1),
        ((1, -1), 0, 1),
        ((-1, 1), 8, 1),
        ((-1, -1), 12, 1),
    ]

    def halo_copy(ref, side, first_of, count, send, recv):
        dz, dy = side
        zs, zt = ranges(dz, 1, cz, 1)
        ys, yt = ranges(dy, ROW, cy, 1)
        group = pl.ds(first_of, count)
        return pltpu.make_async_remote_copy(
            src_ref=ref.at[group, zs, ys, :],
            dst_ref=ref.at[group, zt, yt, :],
            send_sem=send,
            recv_sem=recv,
            device_id=near(split, dz, dy),
            device_id_type=MESH,
        )

    halo = []
    for i, (side, first_of, count) in enumerate(crossing):
        halo.append(halo_copy(post, side, first_of, count, p_send.at[i], p_recv.at[i]))
    for i, side in enumerate(SIDES):
        first_of = 0 if side[1] == 0 else (1 if side[0] == 0 else 1)
        count = 3 if side[0] and side[1] else 4
        halo.append(halo_copy(shear, side, first_of, count, s_send.at[i], s_recv.at[i]))

    for copy in halo:
        copy.start()

    d1r[xc] = d1s[xc]
    for_others(xc, nxc, lambda j: d1_copy(j, j).wait_recv())
    total = d1r[0]
    for j in range(1, nxc):
        total = total + d1r[j]
    d2[z] = total
    for_others(z, nz, lambda j: d2_copy(j, z).start())

    kk, nmark = cell_ref.shape
    nrows = cz * cy
    row_iota = lax.broadcasted_iota(jnp.int32, (nmark, nrows), 1)
    lane_iota = lax.broadcasted_iota(jnp.int32, (nmark, cx), 1)
    cells = jnp.transpose(cell_ref[...], (1, 0))
    weights = jnp.transpose(weight_ref[...], (1, 0))
    for k in range(kk):
        cell = cells[:, k : k + 1]
        line = cell // cx
        block = pl.ds(k * nmark, nmark)
        picked = jnp.where(row_iota == line, 1.0, 0.0).astype(jnp.bfloat16)
        pick[block, 0:nrows] = picked
        pick[block, nrows : 2 * nrows] = picked
        lanes[block, :] = jnp.where(lane_iota == cell - line * cx, weights[:, k : k + 1], 0.0)
    ids = seg_ref[...].reshape(1, nmark)
    lane_count = SEG_DEV * ng2
    seg_iota = lax.broadcasted_iota(jnp.int32, (lane_count, nmark), 0)
    for j in range(ng1):
        hot[j] = jnp.where(seg_iota == ids - j * lane_count, 1.0, 0.0).astype(jnp.bfloat16)

    for_others(z, nz, lambda j: d2_copy(j, j).wait_recv())
    total = d2[0]
    for j in range(1, nz):
        total = total + d2[j]
    d1s[xc] = total
    eddy_rows = jnp.maximum(d1s[xc, 0:rows, :] / (d1s[xc, rows : 2 * rows, :] + eps_sum), 0.0)
    d3[xc, 0:rows, :] = eddy_rows
    d3[xc, rows : 2 * rows, :] = eddy_rows
    for_others(xc, nxc, lambda j: d3_copy(j, xc).start())

    @pl.when(last)
    def _():
        for_all(nxc, lambda j: edge_copy(j, 0).start())

    @pl.when(first)
    def _():
        for_all(nxc, lambda j: edge_copy(j, 1).start())

    for copy in halo:
        copy.wait()
    for_others(xc, nxc, lambda j: d3_copy(j, j).wait_recv())
    for side in range(2):
        edge_copy(0, side).wait_recv()
    for j in range(nxc):
        eddy_ref[j * rows : (j + 1) * rows, :] = d3[j, 0:rows, :]
        eddyx[ROW + j * rows : ROW + (j + 1) * rows, :] = d3[j, 0:rows, :]
    eddyx[ROW - 1 : ROW, :] = dlow[rows - 1 : rows, :]
    eddyx[ROW + cy : ROW + cy + 1, :] = dhigh[0:1, :]

    def relax(p, start, count, which):
        here = pl.ds(start, count)
        mag = mags[p, pl.ds(start - ROW + 1, count), :]
        rate = 1.0 / (0.5 + 3.0 * (base_visc + eddyx[here, :] * mag))
        parts = {}

        def moment(n):
            if n not in parts:
                parts[n] = rate * shear[n, p, here, :]
            return parts[n]

        def lost(n):
            if n in parts:
                return parts[n]
            if n == "y":
                value = moment(XX) + moment(WW)
            elif n == "z":
                value = moment(XX) - moment(WW)
            else:
                value = -2.0 * moment(XX)
            parts[n] = value
            return value

        rules = [
            lambda: 2.0 * moment(XX),
            lambda: moment(WW) - moment(XX),
            lambda: -lost("y"),
            lambda: lost("y") + moment(XY),
            lambda: lost("y") - moment(XY),
            lambda: lost("z") + moment(XZ),
            lambda: lost("z") - moment(XZ),
            lambda: lost("yz") + moment(YZ),
            lambda: lost("yz") - moment(YZ),
        ]
        for q in which:
            value = post[PLACE[q], p, here, :]
            if q:
                pair = (q - 1) // 2
                if ("pair", pair) not in parts:
                    parts["pair", pair] = rules[pair]()
                value = value - parts["pair", pair]
            post[PLACE[q], p, here, :] = value.astype(jnp.bfloat16).astype(jnp.float32)

    def going(dz, dy):
        return [
            q
            for q, (ex, ey, ez) in enumerate(VELOCITIES)
            if (dz == 0 or ez == dz) and (dy == 0 or ey == dy)
        ]

    def finish_plane(i, carry):
        relax(i, ROW, cy, range(19))
        relax(i, ROW - 1, 1, going(0, 1))
        relax(i, ROW + cy, 1, going(0, -1))
        return carry

    lax.fori_loop(1, cz + 1, finish_plane, 0)
    for p, dz in ((0, 1), (cz + 1, -1)):
        relax(p, ROW, cy, going(dz, 0))
        relax(p, ROW - 1, 1, going(dz, 1))
        relax(p, ROW + cy, 1, going(dz, -1))

    def stream_plane(i, carry):
        f = []
        for q, (ex, ey, ez) in enumerate(VELOCITIES):
            value = post[PLACE[q], i + 1 - ez, pl.ds(ROW - ey, cy), :]
            if ex:
                value = roll_x(value, ex)
            outv[q, i] = value.astype(jnp.bfloat16)
            f.append(value)
        d = [f[2 * n + 1] - f[2 * n + 2] for n in range(9)]
        jx = d[0] + (d[3] + d[4]) + (d[5] + d[6])
        jy = d[1] + (d[3] - d[4]) + (d[7] + d[8])
        jz = d[2] + (d[5] - d[6]) + (d[7] - d[8])
        lines = pl.ds(pl.multiple_of(i * cy, cy), cy)
        lower = pl.ds(pl.multiple_of(nrows + i * cy, cy), cy)
        for n, value in enumerate((jx, jy, jz)):
            high = value.astype(jnp.bfloat16)
            low = (value - high.astype(jnp.float32)).astype(jnp.bfloat16)
            mom[lines, n * cx : (n + 1) * cx] = high
            mom[lower, n * cx : (n + 1) * cx] = low
        return carry

    lax.fori_loop(0, cz, stream_plane, 0)

    gath[...] = jnp.dot(pick[...], mom[...], preferred_element_type=jnp.float32)

    def parts_of(value):
        first_part = value.astype(jnp.bfloat16)
        return first_part, (value - first_part.astype(jnp.float32)).astype(jnp.bfloat16)

    def dot_t(a, b):
        return lax.dot_general(a, b, (((1,), (1,)), ((), ())), preferred_element_type=jnp.float32)

    ones = jnp.ones((16, cx), jnp.bfloat16)
    forces = []
    for n in range(3):
        acc = None
        for k in range(kk):
            block = pl.ds(k * nmark, nmark)
            term = lanes[block, :] * gath[block, n * cx : (n + 1) * cx]
            acc = term if acc is None else acc + term
        a, b = parts_of(acc)
        forces.append(-(dot_t(ones, a) + dot_t(ones, b))[0:8])
    which = lax.broadcasted_iota(jnp.int32, (8, nmark), 0)
    force = jnp.where(which == 0, forces[0], jnp.where(which == 1, forces[1], forces[2]))
    a, b = parts_of(force)
    both = jnp.concatenate([a.astype(jnp.float32), b.astype(jnp.float32)], axis=0).astype(jnp.bfloat16)
    for j in range(ng1):
        sums_of = dot_t(both, hot[j])
        h1s[j] = sums_of[0:8] + sums_of[8:16]

    for_others(g1, ng1, lambda j: h1_copy(j, g1).start())
    h1r[g1] = h1s[g1]
    for_others(g1, ng1, lambda j: h1_copy(j, j).wait_recv())
    total = h1r[0]
    for j in range(1, ng1):
        total = total + h1r[j]
    h2[g2] = total
    for_others(g2, ng2, lambda j: h2_copy(j, g2).start())

    for_others(xc, nxc, lambda j: d1_copy(j, xc).wait_send())
    for_others(z, nz, lambda j: d2_copy(j, z).wait_send())
    for_others(xc, nxc, lambda j: d3_copy(j, xc).wait_send())
    for_others(g1, ng1, lambda j: h1_copy(j, g1).wait_send())

    @pl.when(last)
    def _():
        for_all(nxc, lambda j: edge_copy(j, 0).wait_send())

    @pl.when(first)
    def _():
        for_all(nxc, lambda j: edge_copy(j, 1).wait_send())

    for_others(g2, ng2, lambda j: h2_copy(j, j).wait_recv())
    total = h2[0]
    for j in range(1, ng2):
        total = total + h2[j]
    mine = pltpu.roll(total, (lane_count - place * SEG_DEV) % lane_count, axis=1)
    force_ref[...] = mine[0:3, 0:SEG_DEV]
    for_others(g2, ng2, lambda j: h2_copy(j, g2).wait_send())


def write_kernel(outv, eddy, force, out_hbm, eddy_hbm, force_hbm, sem):
    copies = [
        pltpu.make_async_copy(outv, out_hbm, sem.at[0]),
        pltpu.make_async_copy(eddy, eddy_hbm, sem.at[1]),
        pltpu.make_async_copy(force, force_hbm, sem.at[2]),
    ]
    for copy in copies:
        copy.start()
    for copy in copies:
        copy.wait()


def local(split, populations, cell_index, marker_weight, segment_id):
    nq, cz, cy, cx = populations.shape
    nmark, kk = cell_index.shape
    nz, nx, nc, ny = split
    nxc = nx * nc
    ng1, ng2 = nz * (nx // 2), 2 * nc * ny
    rows = cy // nxc
    f32, bf16 = jnp.float32, jnp.bfloat16
    dma = pltpu.SemaphoreType.DMA
    vmem = pl.BlockSpec(memory_space=pltpu.VMEM)
    hbm = pl.BlockSpec(memory_space=pltpu.HBM)
    lane_count = SEG_DEV * ng2
    velocity = pl.pallas_call(
        functools.partial(velocity_kernel, split),
        out_shape=pltpu.VMEM((3, cz + 4, TOP, cx), f32),
        in_specs=[hbm],
        out_specs=vmem,
        scratch_shapes=[
            pltpu.VMEM((nq, cz, cy, cx), bf16),
            dma((4,)),
            dma((8,)),
            dma((8,)),
        ],
        compiler_params=pltpu.CompilerParams(
            collective_id=0, has_side_effects=True, vmem_limit_bytes=8 * 1024 * 1024
        ),
    )(pltpu.with_memory_space_constraint(populations, pltpu.HBM))
    scratch = [
        pltpu.VMEM((3 * cx, cx), bf16),
        pltpu.VMEM((12, cy, cx), f32),
        pltpu.VMEM((12, cy, cx), f32),
        pltpu.VMEM((cz + 2, 40, cx), f32),
        pltpu.VMEM((12, 40, cx), f32),
        pltpu.VMEM((12, 40, cx), f32),
        pltpu.VMEM((3, 48, cx), f32),
        pltpu.VMEM((3, 48, cx), f32),
        pltpu.VMEM((3, cz + 3, 40, cx), f32),
        pltpu.VMEM((12, cz + 4, cy, cx), f32),
        pltpu.VMEM((2, cy, cx), f32),
        pltpu.VMEM((5, cz + 2, TOP, cx), f32),
        pltpu.VMEM((nq, cz + 2, TOP, cx), f32),
        pltpu.VMEM((TOP, cx), f32),
        pltpu.VMEM((2 * cz * cy, 3 * cx), bf16),
        pltpu.VMEM((kk * nmark, 2 * cz * cy), bf16),
        pltpu.VMEM((kk * nmark, cx), f32),
        pltpu.VMEM((kk * nmark, 3 * cx), f32),
        pltpu.VMEM((ng1, lane_count, nmark), bf16),
        pltpu.VMEM((nxc, 2 * rows, cx), f32),
        pltpu.VMEM((nxc, 2 * rows, cx), f32),
        pltpu.VMEM((nz, 2 * rows, cx), f32),
        pltpu.VMEM((nxc, 2 * rows, cx), f32),
        pltpu.VMEM((2 * rows, cx), f32),
        pltpu.VMEM((2 * rows, cx), f32),
        pltpu.VMEM((ng1, 8, lane_count), f32),
        pltpu.VMEM((ng1, 8, lane_count), f32),
        pltpu.VMEM((ng2, 8, lane_count), f32),
        dma((9,)),
        dma((9,)),
        dma((8,)),
        dma((8,)),
        dma((nxc,)),
        dma((nxc,)),
        dma((nz,)),
        dma((nz,)),
        dma((nxc,)),
        dma((nxc,)),
        dma((2, nxc)),
        dma((2,)),
        dma((ng1,)),
        dma((ng1,)),
        dma((ng2,)),
        dma((ng2,)),
    ]
    results = pl.pallas_call(
        functools.partial(step_kernel, split),
        out_shape=(
            pltpu.VMEM((nq, cz, cy, cx), bf16),
            pltpu.VMEM((cy, cx), f32),
            pltpu.VMEM((3, SEG_DEV), f32),
        ),
        in_specs=[vmem, vmem, vmem, vmem, vmem],
        out_specs=(vmem, vmem, vmem),
        scratch_shapes=scratch,
        compiler_params=pltpu.CompilerParams(
            collective_id=1, has_side_effects=True, vmem_limit_bytes=40 * 1024 * 1024
        ),
    )(velocity, populations, cell_index.T, marker_weight.T, segment_id)
    return pl.pallas_call(
        write_kernel,
        out_shape=(
            jax.ShapeDtypeStruct((nq, cz, cy, cx), bf16),
            jax.ShapeDtypeStruct((cy, cx), f32),
            jax.ShapeDtypeStruct((3, SEG_DEV), f32),
        ),
        in_specs=[vmem, vmem, vmem],
        out_specs=(hbm, hbm, hbm),
        scratch_shapes=[dma((3,))],
        compiler_params=pltpu.CompilerParams(vmem_limit_bytes=1024 * 1024),
    )(*results)


def solution(mesh):
    in_specs = (
        P(None, "span", "cross", None),
        P(("span", "cross"), None),
        P(("span", "cross"), None),
        P(("span", "cross")),
    )
    out_specs = (P(None, "span", "cross", None), P("cross", None), P(None, ("span", "cross")))
    sizes = dict(mesh.shape)
    split = (sizes["span"] // (CHIPS_X * CORES), CHIPS_X, CORES, sizes["cross"])
    return jax.shard_map(
        functools.partial(local, split),
        mesh=mesh,
        in_specs=in_specs,
        out_specs=out_specs,
        check_vma=False,
    )
```

time: 66.4 us -> 53.7 us (0.81)
  Pallas kernels: 60.7 us -> 52.9 us
  local copies, waits for them, and re-layouts: 4.86 us -> 0.02 us
    pallas_call x1 -> x3, Pallas kernels: 60.7 us -> 52.9 us  [the longest x1 37.1 us: local(): pl.pallas_call(functools.partial(step_kernel, split), out_shape=(pltpu.VM...]
    unnamed x7 -> x8, local copies, waits for them, and re-layouts: 4.86 us -> 0.02 us
where the time goes in v2:
time: 53.7 us; the launch traced here: 53.6 us
  Pallas kernels  52.9 us (99%)
  between operations  0.71 us (1%)
    pallas_call x1, Pallas kernels, local(): pl.pallas_call(functools.partial(step_kernel, split), out_shape=(pltpu.VM...  37.1 us
    pallas_call x1, Pallas kernels, local(): pl.pallas_call(functools.partial(velocity_kernel, split), out_shape=pltpu...  14.3 us
    pallas_call x1, Pallas kernels, local(): pl.pallas_call(write_kernel, out_shape=(jax.ShapeDtypeStruct((nq, cz, cy,...  1.48 us

profile of v2, /device:TPU:1, one launch (start us, length us, event | category | flops | bytes accessed | tf_op | source)
XLA Modules:
  0.0 53.6 jit_solution(13113184496757700080)
XLA Ops:
  0.6 0.0 copy-start
  0.6 0.0 copy-start.3
  0.7 0.0 copy-start.2
  0.7 0.0 copy-start.1
  0.7 14.3 %shard_map.67.vel = f32[3,20,48,128]{3,2,1,0:T(8,128)S(1)} custom-call(bf16[19,16,32,128]{3,2,1,0:T(8,128)(2,1)} %pops.1), custom_call_target="tpu_custom_call" | custom-call | tf_op jit(solution)/shard_map/pallas_call | solution.py:721
  15.0 0.0 copy-done
  15.0 0.0 copy-done.3
  15.0 0.0 copy-done.2
  15.0 0.0 copy-done.1
  15.0 37.1 %shard_map.68 = (bf16[19,16,32,128]{3,2,1,0:T(8,128)(2,1)S(1)}, f32[32,128]{1,0:T(8,128)S(1)}, f32[3,8]{1,0:T(4,128)S(1)}) custom-call(f32[3,20,48,128]{3,2,1,0:T(8,128)S(1)} %shard_map.67.vel, bf16[19,16,32,128]{3,2,1,0:T(8,128)(2,1)S(1)} %copy-done, s32[8,128]{1,0:T(8,128)S(1)} %bitcast.2, f32[8,128]{1,0:T(8,128)S(1)} %bitcast.3, s32[128]{0:T(128)S(1)} %copy-done.3), custom_call_target="tpu_custom_call" | custom-call | tf_op jit(solution)/shard_map/pallas_call | solution.py:782
  52.1 1.5 %shard_map.69 = (bf16[19,16,32,128]{3,2,1,0:T(8,128)(2,1)}, f32[32,128]{1,0:T(8,128)}, f32[3,8]{1,0:T(4,128)}) custom-call(bf16[19,16,32,128]{3,2,1,0:T(8,128)(2,1)S(1)} %get-tuple-element.6.outv, f32[32,128]{1,0:T(8,128)S(1)} %get-tuple-element.7.eddy, f32[3,8]{1,0:T(4,128)S(1)} %get-tuple-element.8.force), custom_call_target="tpu_custom_call" | custom-call | tf_op jit(solution)/shard_map/pallas_call | solution.py:796
Async XLA Ops:
  0.6 14.4 %copy-start = (bf16[19,16,32,128]{3,2,1,0:T(8,128)(2,1)S(1)}, bf16[19,16,32,128]{3,2,1,0:T(8,128)(2,1)}, u32[]{:S(2)}) copy-start(bf16[19,16,32,128]{3,2,1,0:T(8,128)(2,1)} %pops.1) | copy-start | bytes 7471108
  0.6 14.4 %copy-start.3 = (s32[128]{0:T(128)S(1)}, s32[128]{0:T(128)}, u32[]{:S(2)}) copy-start(s32[128]{0:T(128)} %seg_ref.1) | copy-start | bytes 1540
  0.7 14.4 %copy-start.2 = (f32[128,8]{0,1:T(8,128)S(1)}, f32[128,8]{0,1:T(8,128)}, u32[]{:S(2)}) copy-start(f32[128,8]{0,1:T(8,128)} %param.6) | copy-start | bytes 12292
  0.7 14.4 %copy-start.1 = (s32[128,8]{0,1:T(8,128)S(1)}, s32[128,8]{0,1:T(8,128)}, u32[]{:S(2)}) copy-start(s32[128,8]{0,1:T(8,128)} %param.5) | copy-start | bytes 12292

commit v3 on v2

--- a/solution.py
+++ b/solution.py
@@ -96,7 +96,8 @@
         some = pl.ds(i * step, step)
         return pltpu.make_async_copy(pops_hbm.at[:, some], pops.at[:, some], in_sem.at[i])
 
-    for i in range(nchunk):
+    order = [0, nchunk - 1] + list(range(1, nchunk - 1))
+    for i in order:
         fetch(i).start()
     barrier = pltpu.get_barrier_semaphore()
     for dz, dy in SIDES:
@@ -118,11 +119,9 @@
         vel[2, i + 2, inner, :] = jz * inv
         return carry
 
-    for i in range(nchunk):
+    def moments_of(i):
         fetch(i).wait()
         lax.fori_loop(i * step, (i + 1) * step, moments_plane, 0)
-
-    pl.semaphore_wait(barrier, len(SIDES))
 
     def vel_copy(i):
         dz, dy = SIDES[i]
@@ -137,8 +136,17 @@
             device_id_type=MESH,
         )
 
-    for i in range(len(SIDES)):
-        vel_copy(i).start()
+    for i in order[:2]:
+        moments_of(i)
+    pl.semaphore_wait(barrier, len(SIDES))
+    for i, (dz, dy) in enumerate(SIDES):
+        if dz:
+            vel_copy(i).start()
+    for i in order[2:]:
+        moments_of(i)
+    for i, (dz, dy) in enumerate(SIDES):
+        if not dz:
+            vel_copy(i).start()
     for i in range(len(SIDES)):
         vel_copy(i).wait()
 
@@ -212,25 +220,22 @@
     place = (x % 2) * (nc * ny) + c * ny + y
     y_up, y_down = (y + 1) % ny, (y + ny - 1) % ny
 
-    def xc_dev(j):
-        return (z * nxc + j, y)
-
-    def z_dev(j):
-        return (j * nxc + xc, y)
-
-    def g1_dev(j):
-        return ((j // half) * nxc + ((j % half) * 2 + x % 2) * nc + c, y)
-
-    def g2_dev(j):
-        return (z * nxc + (x // 2) * (2 * nc) + j % (2 * nc), j // (2 * nc))
-
-    def for_others(me, count, act, unroll=False):
-        def body(t, carry):
-            away = count // 2 + (t // 2) * (1 - 2 * (t % 2))
-            act((me + away) % count)
-            return carry
-
-        lax.fori_loop(1, count, body, 0, unroll=unroll)
+    def xc_dev(k):
+        return (s - xc + (xc + k) % nxc, y)
+
+    def z_dev(k):
+        return ((s + nxc * k) % (nz * nxc), y)
+
+    def g1_dev(k):
+        return ((s + 2 * nc * k) % (nz * nxc), y)
+
+    def g2_dev(k):
+        other = (g2 + k) % ng2
+        return (s - s % (2 * nc) + other % (2 * nc), other // (2 * nc))
+
+    def for_others(me, count, act):
+        for k in sorted(range(1, count), key=lambda k: abs(2 * k - count)):
+            act(k, (me + k) % count)
 
     def for_all(count, act):
         def body(j, carry):
@@ -244,10 +249,10 @@
     def greet(dev):
         pl.semaphore_signal(barrier, inc=1, device_id=dev, device_id_type=MESH)
 
-    for_others(g1, ng1, lambda j: greet(g1_dev(j)))
-    for_others(g2, ng2, lambda j: greet(g2_dev(j)))
-    for_others(z, nz, lambda j: greet(z_dev(j)))
-    for_others(xc, nxc, lambda j: greet(xc_dev(j)))
+    for_others(g1, ng1, lambda k, j: greet(g1_dev(k)))
+    for_others(g2, ng2, lambda k, j: greet(g2_dev(k)))
+    for_others(z, nz, lambda k, j: greet(z_dev(k)))
+    for_others(xc, nxc, lambda k, j: greet(xc_dev(k)))
     for dz, dy in SIDES:
         greet(near(split, dz, dy))
     greet((z * nxc + nxc - 1, y_down))
@@ -358,24 +363,24 @@
         d1s[j, 0:rows, :] = sums[0, j * rows : (j + 1) * rows, :]
         d1s[j, rows : 2 * rows, :] = sums[1, j * rows : (j + 1) * rows, :]
 
-    def exchange(src, dst, slot, send, recv, dev, j):
+    def exchange(src, dst, slot, send, recv, dev, k):
         return pltpu.make_async_remote_copy(
             src_ref=src,
             dst_ref=dst.at[slot],
-            send_sem=send.at[j],
+            send_sem=send.at[k],
             recv_sem=recv.at[slot],
-            device_id=dev(j),
+            device_id=dev(k),
             device_id_type=MESH,
         )
 
-    def d1_copy(j, slot):
-        return exchange(d1s.at[j], d1r, slot, d1_send, d1_recv, xc_dev, j)
-
-    def d2_copy(j, slot):
-        return exchange(d2.at[z], d2, slot, d2_send, d2_recv, z_dev, j)
-
-    def d3_copy(j, slot):
-        return exchange(d3.at[xc], d3, slot, d3_send, d3_recv, xc_dev, j)
+    def d1_copy(k, j, slot):
+        return exchange(d1s.at[j], d1r, slot, d1_send, d1_recv, xc_dev, k)
+
+    def d2_copy(k, j, slot):
+        return exchange(d2.at[z], d2, slot, d2_send, d2_recv, z_dev, k)
+
+    def d3_copy(k, j, slot):
+        return exchange(d3.at[xc], d3, slot, d3_send, d3_recv, xc_dev, k)
 
     def edge_copy(j, side):
         return pltpu.make_async_remote_copy(
@@ -387,14 +392,14 @@
             device_id_type=MESH,
         )
 
-    def h1_copy(j, slot):
-        return exchange(h1s.at[j], h1r, slot, h1_send, h1_recv, g1_dev, j)
-
-    def h2_copy(j, slot):
-        return exchange(h2.at[g2], h2, slot, h2_send, h2_recv, g2_dev, j)
+    def h1_copy(k, j, slot):
+        return exchange(h1s.at[j], h1r, slot, h1_send, h1_recv, g1_dev, k)
+
+    def h2_copy(k, j, slot):
+        return exchange(h2.at[g2], h2, slot, h2_send, h2_recv, g2_dev, k)
 
     pl.semaphore_wait(barrier, greeted)
-    for_others(xc, nxc, lambda j: d1_copy(j, xc).start())
+    for_others(xc, nxc, lambda k, j: d1_copy(k, j, xc).start())
 
     inner = pl.ds(ROW, cy)
 
@@ -495,12 +500,12 @@
         copy.start()
 
     d1r[xc] = d1s[xc]
-    for_others(xc, nxc, lambda j: d1_copy(j, j).wait_recv())
+    for_others(xc, nxc, lambda k, j: d1_copy(k, j, j).wait_recv())
     total = d1r[0]
     for j in range(1, nxc):
         total = total + d1r[j]
     d2[z] = total
-    for_others(z, nz, lambda j: d2_copy(j, z).start())
+    for_others(z, nz, lambda k, j: d2_copy(k, j, z).start())
 
     kk, nmark = cell_ref.shape
     nrows = cz * cy
@@ -516,21 +521,23 @@
         pick[block, 0:nrows] = picked
         pick[block, nrows : 2 * nrows] = picked
         lanes[block, :] = jnp.where(lane_iota == cell - line * cx, weights[:, k : k + 1], 0.0)
-    ids = seg_ref[...].reshape(1, nmark)
+    ids = jnp.broadcast_to(seg_ref[...].reshape(1, nmark), (8, nmark))
+    ids = jnp.transpose(ids, (1, 0))[:, 0:1]
     lane_count = SEG_DEV * ng2
-    seg_iota = lax.broadcasted_iota(jnp.int32, (lane_count, nmark), 0)
+    seg_iota = lax.broadcasted_iota(jnp.int32, (nmark, lane_count), 1)
     for j in range(ng1):
-        hot[j] = jnp.where(seg_iota == ids - j * lane_count, 1.0, 0.0).astype(jnp.bfloat16)
-
-    for_others(z, nz, lambda j: d2_copy(j, j).wait_recv())
+        hot[:, j * lane_count : (j + 1) * lane_count] = jnp.where(
+            seg_iota == ids - j * lane_count, 1.0, 0.0
+        ).astype(jnp.bfloat16)
+
+    for_others(z, nz, lambda k, j: d2_copy(k, j, j).wait_recv())
     total = d2[0]
     for j in range(1, nz):
         total = total + d2[j]
     d1s[xc] = total
     eddy_rows = jnp.maximum(d1s[xc, 0:rows, :] / (d1s[xc, rows : 2 * rows, :] + eps_sum), 0.0)
-    d3[xc, 0:rows, :] = eddy_rows
-    d3[xc, rows : 2 * rows, :] = eddy_rows
-    for_others(xc, nxc, lambda j: d3_copy(j, xc).start())
+    d3[xc] = eddy_rows
+    for_others(xc, nxc, lambda k, j: d3_copy(k, j, xc).start())
 
     @pl.when(last)
     def _():
@@ -542,12 +549,12 @@
 
     for copy in halo:
         copy.wait()
-    for_others(xc, nxc, lambda j: d3_copy(j, j).wait_recv())
+    for_others(xc, nxc, lambda k, j: d3_copy(k, j, j).wait_recv())
     for side in range(2):
         edge_copy(0, side).wait_recv()
     for j in range(nxc):
-        eddy_ref[j * rows : (j + 1) * rows, :] = d3[j, 0:rows, :]
-        eddyx[ROW + j * rows : ROW + (j + 1) * rows, :] = d3[j, 0:rows, :]
+        eddy_ref[j * rows : (j + 1) * rows, :] = d3[j]
+        eddyx[ROW + j * rows : ROW + (j + 1) * rows, :] = d3[j]
     eddyx[ROW - 1 : ROW, :] = dlow[rows - 1 : rows, :]
     eddyx[ROW + cy : ROW + cy + 1, :] = dhigh[0:1, :]
 
@@ -607,24 +614,29 @@
         relax(i, ROW + cy, 1, going(0, -1))
         return carry
 
-    lax.fori_loop(1, cz + 1, finish_plane, 0)
+    lax.fori_loop(1, cz + 1, finish_plane, 0, unroll=2)
     for p, dz in ((0, 1), (cz + 1, -1)):
         relax(p, ROW, cy, going(dz, 0))
         relax(p, ROW - 1, 1, going(dz, 1))
         relax(p, ROW + cy, 1, going(dz, -1))
 
-    def stream_plane(i, carry):
-        f = []
-        for q, (ex, ey, ez) in enumerate(VELOCITIES):
-            value = post[PLACE[q], i + 1 - ez, pl.ds(ROW - ey, cy), :]
-            if ex:
-                value = roll_x(value, ex)
-            outv[q, i] = value.astype(jnp.bfloat16)
-            f.append(value)
-        d = [f[2 * n + 1] - f[2 * n + 2] for n in range(9)]
-        jx = d[0] + (d[3] + d[4]) + (d[5] + d[6])
-        jy = d[1] + (d[3] - d[4]) + (d[7] + d[8])
-        jz = d[2] + (d[5] - d[6]) + (d[7] - d[8])
+    def momentum_plane(i, carry):
+        def came(q):
+            ex, ey, ez = VELOCITIES[q]
+            return post[PLACE[q], i + 1 - ez, pl.ds(ROW - ey, cy), :]
+
+        up = {q: came(q) for q in (1, 7, 9, 11, 13)}
+        down = {q: came(q) for q in (2, 8, 10, 12, 14)}
+        east = (up[1] + up[7] + up[9] + up[11] + up[13], up[7] - up[9], up[11] - up[13])
+        west = (
+            down[2] + down[8] + down[10] + down[12] + down[14],
+            down[10] - down[8],
+            down[14] - down[12],
+        )
+        d56, d78 = came(15) - came(16), came(17) - came(18)
+        jx = roll_x(east[0], 1) - roll_x(west[0], -1)
+        jy = (came(3) - came(4)) + (d56 + d78) + (roll_x(east[1], 1) + roll_x(west[1], -1))
+        jz = (came(5) - came(6)) + (d56 - d78) + (roll_x(east[2], 1) + roll_x(west[2], -1))
         lines = pl.ds(pl.multiple_of(i * cy, cy), cy)
         lower = pl.ds(pl.multiple_of(nrows + i * cy, cy), cy)
         for n, value in enumerate((jx, jy, jz)):
@@ -634,7 +646,7 @@
             mom[lower, n * cx : (n + 1) * cx] = low
         return carry
 
-    lax.fori_loop(0, cz, stream_plane, 0)
+    lax.fori_loop(0, cz, momentum_plane, 0, unroll=2)
 
     gath[...] = jnp.dot(pick[...], mom[...], preferred_element_type=jnp.float32)
 
@@ -659,23 +671,34 @@
     force = jnp.where(which == 0, forces[0], jnp.where(which == 1, forces[1], forces[2]))
     a, b = parts_of(force)
     both = jnp.concatenate([a.astype(jnp.float32), b.astype(jnp.float32)], axis=0).astype(jnp.bfloat16)
+    sums_of = jnp.dot(both, hot[...], preferred_element_type=jnp.float32)
+    sums_of = sums_of[0:3] + sums_of[8:11]
     for j in range(ng1):
-        sums_of = dot_t(both, hot[j])
-        h1s[j] = sums_of[0:8] + sums_of[8:16]
-
-    for_others(g1, ng1, lambda j: h1_copy(j, g1).start())
+        h1s[j] = sums_of[:, j * lane_count : (j + 1) * lane_count]
+
+    for_others(g1, ng1, lambda k, j: h1_copy(k, j, g1).start())
     h1r[g1] = h1s[g1]
-    for_others(g1, ng1, lambda j: h1_copy(j, j).wait_recv())
+
+    def stream_plane(i, carry):
+        for q, (ex, ey, ez) in enumerate(VELOCITIES):
+            value = post[PLACE[q], i + 1 - ez, pl.ds(ROW - ey, cy), :]
+            if ex:
+                value = roll_x(value, ex)
+            outv[q, i] = value.astype(jnp.bfloat16)
+        return carry
+
+    lax.fori_loop(0, cz, stream_plane, 0)
+    for_others(g1, ng1, lambda k, j: h1_copy(k, j, j).wait_recv())
     total = h1r[0]
     for j in range(1, ng1):
         total = total + h1r[j]
     h2[g2] = total
-    for_others(g2, ng2, lambda j: h2_copy(j, g2).start())
-
-    for_others(xc, nxc, lambda j: d1_copy(j, xc).wait_send())
-    for_others(z, nz, lambda j: d2_copy(j, z).wait_send())
-    for_others(xc, nxc, lambda j: d3_copy(j, xc).wait_send())
-    for_others(g1, ng1, lambda j: h1_copy(j, g1).wait_send())
+    for_others(g2, ng2, lambda k, j: h2_copy(k, j, g2).start())
+
+    for_others(xc, nxc, lambda k, j: d1_copy(k, j, xc).wait_send())
+    for_others(z, nz, lambda k, j: d2_copy(k, j, z).wait_send())
+    for_others(xc, nxc, lambda k, j: d3_copy(k, j, xc).wait_send())
+    for_others(g1, ng1, lambda k, j: h1_copy(k, j, g1).wait_send())
 
     @pl.when(last)
     def _():
@@ -685,21 +708,24 @@
     def _():
         for_all(nxc, lambda j: edge_copy(j, 1).wait_send())
 
-    for_others(g2, ng2, lambda j: h2_copy(j, j).wait_recv())
+    for_others(g2, ng2, lambda k, j: h2_copy(k, j, j).wait_recv())
     total = h2[0]
     for j in range(1, ng2):
         total = total + h2[j]
     mine = pltpu.roll(total, (lane_count - place * SEG_DEV) % lane_count, axis=1)
-    force_ref[...] = mine[0:3, 0:SEG_DEV]
-    for_others(g2, ng2, lambda j: h2_copy(j, g2).wait_send())
+    force_ref[...] = mine[:, 0:SEG_DEV]
+    for_others(g2, ng2, lambda k, j: h2_copy(k, j, g2).wait_send())
 
 
 def write_kernel(outv, eddy, force, out_hbm, eddy_hbm, force_hbm, sem):
-    copies = [
-        pltpu.make_async_copy(outv, out_hbm, sem.at[0]),
-        pltpu.make_async_copy(eddy, eddy_hbm, sem.at[1]),
-        pltpu.make_async_copy(force, force_hbm, sem.at[2]),
-    ]
+    pieces = sem.shape[0] - 2
+    step = -(-outv.shape[0] // pieces)
+    copies = []
+    for i in range(pieces):
+        some = pl.ds(i * step, min(step, outv.shape[0] - i * step))
+        copies.append(pltpu.make_async_copy(outv.at[some], out_hbm.at[some], sem.at[i]))
+    copies.append(pltpu.make_async_copy(eddy, eddy_hbm, sem.at[pieces]))
+    copies.append(pltpu.make_async_copy(force, force_hbm, sem.at[pieces + 1]))
     for copy in copies:
         copy.start()
     for copy in copies:
@@ -718,13 +744,15 @@
     vmem = pl.BlockSpec(memory_space=pltpu.VMEM)
     hbm = pl.BlockSpec(memory_space=pltpu.HBM)
     lane_count = SEG_DEV * ng2
-    velocity = pl.pallas_call(
+    velocity, pops = pl.pallas_call(
         functools.partial(velocity_kernel, split),
-        out_shape=pltpu.VMEM((3, cz + 4, TOP, cx), f32),
+        out_shape=(
+            pltpu.VMEM((3, cz + 4, TOP, cx), f32),
+            pltpu.VMEM((nq, cz, cy, cx), bf16),
+        ),
         in_specs=[hbm],
-        out_specs=vmem,
+        out_specs=(vmem, vmem),
         scratch_shapes=[
-            pltpu.VMEM((nq, cz, cy, cx), bf16),
             dma((4,)),
             dma((8,)),
             dma((8,)),
@@ -752,16 +780,16 @@
         pltpu.VMEM((kk * nmark, 2 * cz * cy), bf16),
         pltpu.VMEM((kk * nmark, cx), f32),
         pltpu.VMEM((kk * nmark, 3 * cx), f32),
-        pltpu.VMEM((ng1, lane_count, nmark), bf16),
+        pltpu.VMEM((nmark, ng1 * lane_count), bf16),
         pltpu.VMEM((nxc, 2 * rows, cx), f32),
         pltpu.VMEM((nxc, 2 * rows, cx), f32),
         pltpu.VMEM((nz, 2 * rows, cx), f32),
-        pltpu.VMEM((nxc, 2 * rows, cx), f32),
-        pltpu.VMEM((2 * rows, cx), f32),
-        pltpu.VMEM((2 * rows, cx), f32),
-        pltpu.VMEM((ng1, 8, lane_count), f32),
-        pltpu.VMEM((ng1, 8, lane_count), f32),
-        pltpu.VMEM((ng2, 8, lane_count), f32),
+        pltpu.VMEM((nxc, rows, cx), f32),
+        pltpu.VMEM((rows, cx), f32),
+        pltpu.VMEM((rows, cx), f32),
+        pltpu.VMEM((ng1, 3, lane_count), f32),
+        pltpu.VMEM((ng1, 3, lane_count), f32),
+        pltpu.VMEM((ng2, 3, lane_count), f32),
         dma((9,)),
         dma((9,)),
         dma((8,)),
@@ -792,7 +820,7 @@
         compiler_params=pltpu.CompilerParams(
             collective_id=1, has_side_effects=True, vmem_limit_bytes=40 * 1024 * 1024
         ),
-    )(velocity, populations, cell_index.T, marker_weight.T, segment_id)
+    )(velocity, pops, cell_index.T, marker_weight.T, segment_id)
     return pl.pallas_call(
         write_kernel,
         out_shape=(
@@ -802,7 +830,7 @@
         ),
         in_specs=[vmem, vmem, vmem],
         out_specs=(hbm, hbm, hbm),
-        scratch_shapes=[dma((3,))],
+        scratch_shapes=[dma((6,))],
         compiler_params=pltpu.CompilerParams(vmem_limit_bytes=1024 * 1024),
     )(*results)
 

time: 53.7 us -> 50.7 us (0.944)
  Pallas kernels: 52.9 us -> 49.9 us
    pallas_call x1, Pallas kernels: 37.1 us -> 34.6 us  [local(): pl.pallas_call(functools.partial(step_kernel, split), out_shape=(pltpu.VM...]
where the time goes in v3:
time: 50.7 us; the launch traced here: 50.6 us
  Pallas kernels  49.9 us (98%)
  between operations  0.69 us (1%)
    pallas_call x1, Pallas kernels, local(): pl.pallas_call(functools.partial(step_kernel, split), out_shape=(pltpu.VM...  34.6 us
    pallas_call x1, Pallas kernels, local(): pl.pallas_call(functools.partial(velocity_kernel, split), out_shape=(pltp...  13.8 us
    pallas_call x1, Pallas kernels, local(): pl.pallas_call(write_kernel, out_shape=(jax.ShapeDtypeStruct((nq, cz, cy,...  1.5 us

profile of v3, /device:TPU:1, one launch (start us, length us, event | category | flops | bytes accessed | tf_op | source)
XLA Modules:
  0.0 50.6 jit_solution(13226982698804838328)
XLA Ops:
  0.6 0.0 copy-start.2
  0.6 0.0 copy-start.1
  0.7 0.0 copy-start
  0.7 13.8 %shard_map.67 = (f32[3,20,48,128]{3,2,1,0:T(8,128)S(1)}, bf16[19,16,32,128]{3,2,1,0:T(8,128)(2,1)S(1)}) custom-call(bf16[19,16,32,128]{3,2,1,0:T(8,128)(2,1)} %pops_hbm.1), custom_call_target="tpu_custom_call" | custom-call | tf_op jit(solution)/shard_map/pallas_call | solution.py:747
  14.5 0.0 copy-done.2
  14.5 0.0 copy-done.1
  14.5 0.0 copy-done
  14.5 34.6 %shard_map.68 = (bf16[19,16,32,128]{3,2,1,0:T(8,128)(2,1)S(1)}, f32[32,128]{1,0:T(8,128)S(1)}, f32[3,8]{1,0:T(4,128)S(1)}) custom-call(f32[3,20,48,128]{3,2,1,0:T(8,128)S(1)} %get-tuple-element.8.vel, bf16[19,16,32,128]{3,2,1,0:T(8,128)(2,1)S(1)} %get-tuple-element.9.pops, s32[8,128]{1,0:T(8,128)S(1)} %bitcast.2, f32[8,128]{1,0:T(8,128)S(1)} %bitcast.3, ...), custom_call_target="tpu_custom_call" | custom-call | tf_op jit(solution)/shard_map/pallas_call | solution.py:810
  49.1 1.5 %shard_map.69 = (bf16[19,16,32,128]{3,2,1,0:T(8,128)(2,1)}, f32[32,128]{1,0:T(8,128)}, f32[3,8]{1,0:T(4,128)}) custom-call(bf16[19,16,32,128]{3,2,1,0:T(8,128)(2,1)S(1)} %get-tuple-element.10.outv, f32[32,128]{1,0:T(8,128)S(1)} %get-tuple-element.11.eddy, f32[3,8]{1,0:T(4,128)S(1)} %get-tuple-element.12.force), custom_call_target="tpu_custom_call" | custom-call | tf_op jit(solution)/shard_map/pallas_call | solution.py:824
Async XLA Ops:
  0.6 13.8 %copy-start.2 = (s32[128]{0:T(128)S(1)}, s32[128]{0:T(128)}, u32[]{:S(2)}) copy-start(s32[128]{0:T(128)} %seg_ref.1) | copy-start | bytes 1540
  0.6 13.8 %copy-start.1 = (f32[128,8]{0,1:T(8,128)S(1)}, f32[128,8]{0,1:T(8,128)}, u32[]{:S(2)}) copy-start(f32[128,8]{0,1:T(8,128)} %param.6) | copy-start | bytes 12292
  0.7 13.8 %copy-start = (s32[128,8]{0,1:T(8,128)S(1)}, s32[128,8]{0,1:T(8,128)}, u32[]{:S(2)}) copy-start(s32[128,8]{0,1:T(8,128)} %param.5) | copy-start | bytes 12292

commit v4 on v3

--- a/solution.py
+++ b/solution.py
@@ -193,18 +193,13 @@
     p_recv,
     s_send,
     s_recv,
-    d1_send,
-    d1_recv,
-    d2_send,
-    d2_recv,
-    d3_send,
-    d3_recv,
+    d1_sem,
+    d2_sem,
+    d3_sem,
     e_send,
     e_recv,
-    h1_send,
-    h1_recv,
-    h2_send,
-    h2_recv,
+    h1_sem,
+    h2_sem,
 ):
     nz, nx, nc, ny = split
     nxc = nx * nc
@@ -363,43 +358,59 @@
         d1s[j, 0:rows, :] = sums[0, j * rows : (j + 1) * rows, :]
         d1s[j, rows : 2 * rows, :] = sums[1, j * rows : (j + 1) * rows, :]
 
-    def exchange(src, dst, slot, send, recv, dev, k):
-        return pltpu.make_async_remote_copy(
-            src_ref=src,
-            dst_ref=dst.at[slot],
-            send_sem=send.at[k],
-            recv_sem=recv.at[slot],
-            device_id=dev(k),
-            device_id_type=MESH,
-        )
-
-    def d1_copy(k, j, slot):
-        return exchange(d1s.at[j], d1r, slot, d1_send, d1_recv, xc_dev, k)
-
-    def d2_copy(k, j, slot):
-        return exchange(d2.at[z], d2, slot, d2_send, d2_recv, z_dev, k)
-
-    def d3_copy(k, j, slot):
-        return exchange(d3.at[xc], d3, slot, d3_send, d3_recv, xc_dev, k)
+    class Exchange:
+        def __init__(self, src, dst, me, count, dev, sems, own):
+            self.src, self.dst, self.me, self.count, self.dev = src, dst, me, count, dev
+            self.sems, self.own = sems, own
+
+        def copy(self, src, dst, k):
+            return pltpu.make_async_remote_copy(
+                src_ref=src,
+                dst_ref=dst,
+                send_sem=self.sems.at[0],
+                recv_sem=self.sems.at[1],
+                device_id=self.dev(k),
+                device_id_type=MESH,
+            )
+
+        def start(self):
+            def send(k, j):
+                self.copy(self.src.at[self.me if self.own else j], self.dst.at[self.me], k).start()
+
+            for_others(self.me, self.count, send)
+
+        def all_of(self):
+            some = pl.ds(0, self.count - 1)
+            return self.copy(self.src.at[some], self.dst.at[some], 1)
+
+    d1x = Exchange(d1s, d1r, xc, nxc, xc_dev, d1_sem, False)
+    d2x = Exchange(d2, d2, z, nz, z_dev, d2_sem, True)
+    d3x = Exchange(d3, d3, xc, nxc, xc_dev, d3_sem, True)
+    h1x = Exchange(h1s, h1r, g1, ng1, g1_dev, h1_sem, False)
+    h2x = Exchange(h2, h2, g2, ng2, g2_dev, h2_sem, True)
 
     def edge_copy(j, side):
         return pltpu.make_async_remote_copy(
             src_ref=d3.at[xc],
             dst_ref=dlow if side == 0 else dhigh,
-            send_sem=e_send.at[side, j],
+            send_sem=e_send.at[side],
             recv_sem=e_recv.at[side],
             device_id=(z * nxc + j, y_up if side == 0 else y_down),
             device_id_type=MESH,
         )
 
-    def h1_copy(k, j, slot):
-        return exchange(h1s.at[j], h1r, slot, h1_send, h1_recv, g1_dev, k)
-
-    def h2_copy(k, j, slot):
-        return exchange(h2.at[g2], h2, slot, h2_send, h2_recv, g2_dev, k)
+    def edges_sent(side):
+        pltpu.make_async_remote_copy(
+            src_ref=d3,
+            dst_ref=d3,
+            send_sem=e_send.at[side],
+            recv_sem=e_recv.at[side],
+            device_id=(z * nxc, y_up),
+            device_id_type=MESH,
+        ).wait_send()
 
     pl.semaphore_wait(barrier, greeted)
-    for_others(xc, nxc, lambda k, j: d1_copy(k, j, xc).start())
+    d1x.start()
 
     inner = pl.ds(ROW, cy)
 
@@ -500,12 +511,12 @@
         copy.start()
 
     d1r[xc] = d1s[xc]
-    for_others(xc, nxc, lambda k, j: d1_copy(k, j, j).wait_recv())
+    d1x.all_of().wait_recv()
     total = d1r[0]
     for j in range(1, nxc):
         total = total + d1r[j]
     d2[z] = total
-    for_others(z, nz, lambda k, j: d2_copy(k, j, z).start())
+    d2x.start()
 
     kk, nmark = cell_ref.shape
     nrows = cz * cy
@@ -530,14 +541,14 @@
             seg_iota == ids - j * lane_count, 1.0, 0.0
         ).astype(jnp.bfloat16)
 
-    for_others(z, nz, lambda k, j: d2_copy(k, j, j).wait_recv())
+    d2x.all_of().wait_recv()
     total = d2[0]
     for j in range(1, nz):
         total = total + d2[j]
     d1s[xc] = total
     eddy_rows = jnp.maximum(d1s[xc, 0:rows, :] / (d1s[xc, rows : 2 * rows, :] + eps_sum), 0.0)
     d3[xc] = eddy_rows
-    for_others(xc, nxc, lambda k, j: d3_copy(k, j, xc).start())
+    d3x.start()
 
     @pl.when(last)
     def _():
@@ -549,7 +560,7 @@
 
     for copy in halo:
         copy.wait()
-    for_others(xc, nxc, lambda k, j: d3_copy(k, j, j).wait_recv())
+    d3x.all_of().wait_recv()
     for side in range(2):
         edge_copy(0, side).wait_recv()
     for j in range(nxc):
@@ -676,7 +687,7 @@
     for j in range(ng1):
         h1s[j] = sums_of[:, j * lane_count : (j + 1) * lane_count]
 
-    for_others(g1, ng1, lambda k, j: h1_copy(k, j, g1).start())
+    h1x.start()
     h1r[g1] = h1s[g1]
 
     def stream_plane(i, carry):
@@ -688,33 +699,33 @@
         return carry
 
     lax.fori_loop(0, cz, stream_plane, 0)
-    for_others(g1, ng1, lambda k, j: h1_copy(k, j, j).wait_recv())
+    h1x.all_of().wait_recv()
     total = h1r[0]
     for j in range(1, ng1):
         total = total + h1r[j]
     h2[g2] = total
-    for_others(g2, ng2, lambda k, j: h2_copy(k, j, g2).start())
-
-    for_others(xc, nxc, lambda k, j: d1_copy(k, j, xc).wait_send())
-    for_others(z, nz, lambda k, j: d2_copy(k, j, z).wait_send())
-    for_others(xc, nxc, lambda k, j: d3_copy(k, j, xc).wait_send())
-    for_others(g1, ng1, lambda k, j: h1_copy(k, j, g1).wait_send())
+    h2x.start()
+
+    d1x.all_of().wait_send()
+    d2x.all_of().wait_send()
+    d3x.all_of().wait_send()
+    h1x.all_of().wait_send()
 
     @pl.when(last)
     def _():
-        for_all(nxc, lambda j: edge_copy(j, 0).wait_send())
+        edges_sent(0)
 
     @pl.when(first)
     def _():
-        for_all(nxc, lambda j: edge_copy(j, 1).wait_send())
-
-    for_others(g2, ng2, lambda k, j: h2_copy(k, j, j).wait_recv())
+        edges_sent(1)
+
+    h2x.all_of().wait_recv()
     total = h2[0]
     for j in range(1, ng2):
         total = total + h2[j]
     mine = pltpu.roll(total, (lane_count - place * SEG_DEV) % lane_count, axis=1)
     force_ref[...] = mine[:, 0:SEG_DEV]
-    for_others(g2, ng2, lambda k, j: h2_copy(k, j, g2).wait_send())
+    h2x.all_of().wait_send()
 
 
 def write_kernel(outv, eddy, force, out_hbm, eddy_hbm, force_hbm, sem):
@@ -794,18 +805,13 @@
         dma((9,)),
         dma((8,)),
         dma((8,)),
-        dma((nxc,)),
-        dma((nxc,)),
-        dma((nz,)),
-        dma((nz,)),
-        dma((nxc,)),
-        dma((nxc,)),
-        dma((2, nxc)),
         dma((2,)),
-        dma((ng1,)),
-        dma((ng1,)),
-        dma((ng2,)),
-        dma((ng2,)),
+        dma((2,)),
+        dma((2,)),
+        dma((2,)),
+        dma((2,)),
+        dma((2,)),
+        dma((2,)),
     ]
     results = pl.pallas_call(
         functools.partial(step_kernel, split),

time: 50.7 us -> 49.6 us (0.978)
  Pallas kernels: 49.9 us -> 48.8 us
    pallas_call x1, Pallas kernels: 34.6 us -> 33.5 us  [local(): pl.pallas_call(functools.partial(step_kernel, split), out_shape=(pltpu.VM...]
where the time goes in v4:
time: 49.6 us; the launch traced here: 49.5 us
  Pallas kernels  48.8 us (98%)
  between operations  0.69 us (1%)
    pallas_call x1, Pallas kernels, local(): pl.pallas_call(functools.partial(step_kernel, split), out_shape=(pltpu.VM...  33.5 us
    pallas_call x1, Pallas kernels, local(): pl.pallas_call(functools.partial(velocity_kernel, split), out_shape=(pltp...  13.8 us
    pallas_call x1, Pallas kernels, local(): pl.pallas_call(write_kernel, out_shape=(jax.ShapeDtypeStruct((nq, cz, cy,...  1.5 us

profile of v4, /device:TPU:1, one launch (start us, length us, event | category | flops | bytes accessed | tf_op | source)
XLA Modules:
  0.0 49.5 jit_solution(9474035703757146768)
XLA Ops:
  0.6 0.0 copy-start.2
  0.6 0.0 copy-start.1
  0.7 0.0 copy-start
  0.7 13.8 %shard_map.67 = (f32[3,20,48,128]{3,2,1,0:T(8,128)S(1)}, bf16[19,16,32,128]{3,2,1,0:T(8,128)(2,1)S(1)}) custom-call(bf16[19,16,32,128]{3,2,1,0:T(8,128)(2,1)} %pops_hbm.1), custom_call_target="tpu_custom_call" | custom-call | tf_op jit(solution)/shard_map/pallas_call | solution.py:758
  14.5 0.0 copy-done.2
  14.5 0.0 copy-done.1
  14.5 0.0 copy-done
  14.5 33.5 %shard_map.68 = (bf16[19,16,32,128]{3,2,1,0:T(8,128)(2,1)S(1)}, f32[32,128]{1,0:T(8,128)S(1)}, f32[3,8]{1,0:T(4,128)S(1)}) custom-call(f32[3,20,48,128]{3,2,1,0:T(8,128)S(1)} %get-tuple-element.8.vel, bf16[19,16,32,128]{3,2,1,0:T(8,128)(2,1)S(1)} %get-tuple-element.9.pops, s32[8,128]{1,0:T(8,128)S(1)} %bitcast.2, f32[8,128]{1,0:T(8,128)S(1)} %bitcast.3, ...), custom_call_target="tpu_custom_call" | custom-call | tf_op jit(solution)/shard_map/pallas_call | solution.py:816
  48.0 1.5 %shard_map.69 = (bf16[19,16,32,128]{3,2,1,0:T(8,128)(2,1)}, f32[32,128]{1,0:T(8,128)}, f32[3,8]{1,0:T(4,128)}) custom-call(bf16[19,16,32,128]{3,2,1,0:T(8,128)(2,1)S(1)} %get-tuple-element.10.outv, f32[32,128]{1,0:T(8,128)S(1)} %get-tuple-element.11.eddy, f32[3,8]{1,0:T(4,128)S(1)} %get-tuple-element.12.force), custom_call_target="tpu_custom_call" | custom-call | tf_op jit(solution)/shard_map/pallas_call | solution.py:830
Async XLA Ops:
  0.6 13.8 %copy-start.2 = (s32[128]{0:T(128)S(1)}, s32[128]{0:T(128)}, u32[]{:S(2)}) copy-start(s32[128]{0:T(128)} %seg_ref.1) | copy-start | bytes 1540
  0.6 13.8 %copy-start.1 = (f32[128,8]{0,1:T(8,128)S(1)}, f32[128,8]{0,1:T(8,128)}, u32[]{:S(2)}) copy-start(f32[128,8]{0,1:T(8,128)} %param.6) | copy-start | bytes 12292
  0.7 13.8 %copy-start = (s32[128,8]{0,1:T(8,128)S(1)}, s32[128,8]{0,1:T(8,128)}, u32[]{:S(2)}) copy-start(s32[128,8]{0,1:T(8,128)} %param.5) | copy-start | bytes 12292

commit v5 on v4

--- a/solution.py
+++ b/solution.py
@@ -87,6 +87,11 @@
     return pl.ds(first, width), pl.ds(first + size, width)
 
 
+def kind(i):
+    dz, dy = SIDES[i]
+    return 2 if dz and dy else (0 if dz else 1)
+
+
 def velocity_kernel(split, pops_hbm, vel, pops, in_sem, v_send, v_recv):
     cz, cy, cx = pops.shape[1:]
     nchunk = in_sem.shape[0]
@@ -130,8 +135,8 @@
         return pltpu.make_async_remote_copy(
             src_ref=vel.at[:, zs, ys, :],
             dst_ref=vel.at[:, zt, yt, :],
-            send_sem=v_send.at[i],
-            recv_sem=v_recv.at[i],
+            send_sem=v_send.at[kind(i)],
+            recv_sem=v_recv.at[kind(i)],
             device_id=near(split, dz, dy),
             device_id_type=MESH,
         )
@@ -147,8 +152,21 @@
     for i, (dz, dy) in enumerate(SIDES):
         if not dz:
             vel_copy(i).start()
-    for i in range(len(SIDES)):
-        vel_copy(i).wait()
+    inner = pl.ds(ROW, cy)
+    wholes = [
+        vel.at[:, pl.ds(0, 4), inner, :],
+        vel.at[:, pl.ds(2, cz), pl.ds(ROW, 4), :],
+        vel.at[:, pl.ds(0, 8), pl.ds(ROW, 2), :],
+    ]
+    for n, whole in enumerate(wholes):
+        pltpu.make_async_remote_copy(
+            src_ref=whole,
+            dst_ref=whole,
+            send_sem=v_send.at[n],
+            recv_sem=v_recv.at[n],
+            device_id=near(split, 0, 1),
+            device_id_type=MESH,
+        ).wait()
 
 
 def step_kernel(
@@ -191,8 +209,6 @@
     h2,
     p_send,
     p_recv,
-    s_send,
-    s_recv,
     d1_sem,
     d2_sem,
     d3_sem,
@@ -246,31 +262,34 @@
 
     for_others(g1, ng1, lambda k, j: greet(g1_dev(k)))
     for_others(g2, ng2, lambda k, j: greet(g2_dev(k)))
-    for_others(z, nz, lambda k, j: greet(z_dev(k)))
-    for_others(xc, nxc, lambda k, j: greet(xc_dev(k)))
-    for dz, dy in SIDES:
+    for k in range(1, half):
+        for t in range(2 * nc):
+            greet((z * nxc + ((x // 2 + k) % half) * (2 * nc) + t, y))
+    beside_span = [side for side in SIDES if side[0]]
+    for dz, dy in beside_span:
         greet(near(split, dz, dy))
     greet((z * nxc + nxc - 1, y_down))
     greet((z * nxc, y_up))
     last, first = xc == nxc - 1, xc == 0
-    greeted = len(SIDES) + (nxc - 1) + (nz - 1) + (ng1 - 1) + (ng2 - 1)
+    greeted = len(beside_span) + (half - 1) * 2 * nc + (ng1 - 1) + (ng2 - 1)
     greeted = greeted + jnp.where(jnp.logical_or(last, first), nxc, 0)
 
     apart = lax.broadcasted_iota(jnp.int32, (cx, cx), 0) - lax.broadcasted_iota(jnp.int32, (cx, cx), 1)
     apart = (apart + cx) % cx
     beside = jnp.logical_or(apart == 1, apart == cx - 1)
-    circulant = jnp.where(apart == 0, 2.0, jnp.where(beside, 1.0, 0.0)).astype(jnp.bfloat16)
+    circulant = jnp.where(apart == 0, 2.0 / 64.0, jnp.where(beside, 1.0 / 64.0, 0.0)).astype(jnp.bfloat16)
     for n in range(3):
         smoother[n * cx : (n + 1) * cx, :] = circulant
 
-    def smooth_x(values):
-        both = jnp.concatenate(values, axis=0)
-        high = both.astype(jnp.bfloat16)
-        rest = both - high.astype(jnp.float32)
-        mid = rest.astype(jnp.bfloat16)
-        low = (rest - mid.astype(jnp.float32)).astype(jnp.bfloat16)
-        parts = jnp.concatenate([high, mid, low], axis=1)
-        return jnp.dot(parts, smoother[...], preferred_element_type=jnp.float32)
+    def smooth_x(values, count=3):
+        rest = jnp.concatenate(values, axis=0)
+        parts = []
+        for n in range(count):
+            parts.append(rest.astype(jnp.bfloat16))
+            if n < count - 1:
+                rest = rest - parts[-1].astype(jnp.float32)
+        parts = jnp.concatenate(parts, axis=1)
+        return jnp.dot(parts, smoother[0 : count * cx, :], preferred_element_type=jnp.float32)
 
     def products(p, tmp, vtmp):
         mid, low, high = pl.ds(ROW - 1, 40), pl.ds(ROW - 2, 40), pl.ds(ROW, 40)
@@ -298,7 +317,7 @@
         along_y = [tri(vtmp[a, 0:40, :], vtmp[a, 1:41, :], vtmp[a, 2:42, :]) for a in range(3)]
         smoothed = smooth_x(along_y)
         for a in range(3):
-            vhat[a, p + 1] = (1.0 / 64.0) * smoothed[a * 40 : (a + 1) * 40]
+            vhat[a, p + 1] = smoothed[a * 40 : (a + 1) * 40]
 
     def two_planes(i, carry):
         products(2 * i, tmp_a, vtmp_a)
@@ -311,10 +330,12 @@
     filters(cz + 1, tmp_b, vtmp_b)
 
     def hats_of(i, hats):
-        along_z = [tri(filt[n, i + 1], filt[n, i + 2], filt[n, i + 3]) for n in range(12)]
-        smoothed = smooth_x(along_z)
-        for n in range(12):
-            hats[n] = (1.0 / 64.0) * smoothed[n * cy : (n + 1) * cy]
+        for first_of, parts in ((0, 2), (6, 3)):
+            fields = range(first_of, first_of + 6)
+            along_z = [tri(filt[n, i + 1], filt[n, i + 2], filt[n, i + 3]) for n in fields]
+            smoothed = smooth_x(along_z, parts)
+            for n in fields:
+                hats[n] = smoothed[(n - first_of) * cy : (n - first_of + 1) * cy]
 
     def add_plane(i, hats, plane_lm, plane_mm):
         mid, low, high = pl.ds(1, cy), pl.ds(0, cy), pl.ds(2, cy)
@@ -500,12 +521,14 @@
         )
 
     halo = []
-    for i, (side, first_of, count) in enumerate(crossing):
-        halo.append(halo_copy(post, side, first_of, count, p_send.at[i], p_recv.at[i]))
+    for side, first_of, count in crossing:
+        n = kind(SIDES.index(side))
+        halo.append(halo_copy(post, side, first_of, count, p_send.at[n], p_recv.at[n]))
     for i, side in enumerate(SIDES):
         first_of = 0 if side[1] == 0 else (1 if side[0] == 0 else 1)
         count = 3 if side[0] and side[1] else 4
-        halo.append(halo_copy(shear, side, first_of, count, s_send.at[i], s_recv.at[i]))
+        n = 3 + kind(i)
+        halo.append(halo_copy(shear, side, first_of, count, p_send.at[n], p_recv.at[n]))
 
     for copy in halo:
         copy.start()
@@ -520,7 +543,8 @@
 
     kk, nmark = cell_ref.shape
     nrows = cz * cy
-    row_iota = lax.broadcasted_iota(jnp.int32, (nmark, nrows), 1)
+    nhalf = nrows // 2
+    row_iota = lax.broadcasted_iota(jnp.int32, (nmark, nhalf), 1)
     lane_iota = lax.broadcasted_iota(jnp.int32, (nmark, cx), 1)
     cells = jnp.transpose(cell_ref[...], (1, 0))
     weights = jnp.transpose(weight_ref[...], (1, 0))
@@ -528,9 +552,10 @@
         cell = cells[:, k : k + 1]
         line = cell // cx
         block = pl.ds(k * nmark, nmark)
-        picked = jnp.where(row_iota == line, 1.0, 0.0).astype(jnp.bfloat16)
-        pick[block, 0:nrows] = picked
-        pick[block, nrows : 2 * nrows] = picked
+        for h in range(2):
+            picked = jnp.where(row_iota == line - h * nhalf, 1.0, 0.0).astype(jnp.bfloat16)
+            pick[block, h * nrows : h * nrows + nhalf] = picked
+            pick[block, h * nrows + nhalf : (h + 1) * nrows] = picked
         lanes[block, :] = jnp.where(lane_iota == cell - line * cx, weights[:, k : k + 1], 0.0)
     ids = jnp.broadcast_to(seg_ref[...].reshape(1, nmark), (8, nmark))
     ids = jnp.transpose(ids, (1, 0))[:, 0:1]
@@ -558,8 +583,23 @@
     def _():
         for_all(nxc, lambda j: edge_copy(j, 1).start())
 
-    for copy in halo:
-        copy.wait()
+    wholes = [
+        post.at[pl.ds(0, 10), pl.ds(1, 1), inner, :],
+        post.at[pl.ds(0, 10), pl.ds(1, cz), pl.ds(ROW, 1), :],
+        post.at[pl.ds(0, 4), pl.ds(1, 1), pl.ds(ROW, 1), :],
+        shear.at[pl.ds(0, 4), pl.ds(1, 2), inner, :],
+        shear.at[pl.ds(0, 4), pl.ds(1, cz), pl.ds(ROW, 2), :],
+        shear.at[pl.ds(0, 3), pl.ds(1, 4), pl.ds(ROW, 1), :],
+    ]
+    for n, whole in enumerate(wholes):
+        pltpu.make_async_remote_copy(
+            src_ref=whole,
+            dst_ref=whole,
+            send_sem=p_send.at[n],
+            recv_sem=p_recv.at[n],
+            device_id=near(split, 0, 1),
+            device_id_type=MESH,
+        ).wait()
     d3x.all_of().wait_recv()
     for side in range(2):
         edge_copy(0, side).wait_recv()
@@ -625,13 +665,13 @@
         relax(i, ROW + cy, 1, going(0, -1))
         return carry
 
-    lax.fori_loop(1, cz + 1, finish_plane, 0, unroll=2)
+    lax.fori_loop(1, cz + 1, finish_plane, 0, unroll=4)
     for p, dz in ((0, 1), (cz + 1, -1)):
         relax(p, ROW, cy, going(dz, 0))
         relax(p, ROW - 1, 1, going(dz, 1))
         relax(p, ROW + cy, 1, going(dz, -1))
 
-    def momentum_plane(i, carry):
+    def momentum_plane(h, i):
         def came(q):
             ex, ey, ez = VELOCITIES[q]
             return post[PLACE[q], i + 1 - ez, pl.ds(ROW - ey, cy), :]
@@ -648,18 +688,30 @@
         jx = roll_x(east[0], 1) - roll_x(west[0], -1)
         jy = (came(3) - came(4)) + (d56 + d78) + (roll_x(east[1], 1) + roll_x(west[1], -1))
         jz = (came(5) - came(6)) + (d56 - d78) + (roll_x(east[2], 1) + roll_x(west[2], -1))
-        lines = pl.ds(pl.multiple_of(i * cy, cy), cy)
-        lower = pl.ds(pl.multiple_of(nrows + i * cy, cy), cy)
+        line = (i - h * (cz // 2)) * cy + h * nrows
+        if not isinstance(line, int):
+            line = pl.multiple_of(line, cy)
+        lines, lower = pl.ds(line, cy), pl.ds(line + nhalf, cy)
         for n, value in enumerate((jx, jy, jz)):
             high = value.astype(jnp.bfloat16)
             low = (value - high.astype(jnp.float32)).astype(jnp.bfloat16)
             mom[lines, n * cx : (n + 1) * cx] = high
             mom[lower, n * cx : (n + 1) * cx] = low
+
+    def first_half(i, carry):
+        momentum_plane(0, i)
         return carry
 
-    lax.fori_loop(0, cz, momentum_plane, 0, unroll=2)
-
-    gath[...] = jnp.dot(pick[...], mom[...], preferred_element_type=jnp.float32)
+    lax.fori_loop(0, cz // 2, first_half, 0, unroll=min(4, cz // 2))
+
+    def gathered(h):
+        lines = pl.ds(h * nrows, nrows)
+        return jnp.dot(pick[:, lines], mom[lines, :], preferred_element_type=jnp.float32)
+
+    gath[0] = gathered(0)
+    for i in range(cz // 2, cz):
+        momentum_plane(1, i)
+    gath[1] = gathered(1)
 
     def parts_of(value):
         first_part = value.astype(jnp.bfloat16)
@@ -674,7 +726,8 @@
         acc = None
         for k in range(kk):
             block = pl.ds(k * nmark, nmark)
-            term = lanes[block, :] * gath[block, n * cx : (n + 1) * cx]
+            here = pl.ds(n * cx, cx)
+            term = lanes[block, :] * (gath[0, block, here] + gath[1, block, here])
             acc = term if acc is None else acc + term
         a, b = parts_of(acc)
         forces.append(-(dot_t(ones, a) + dot_t(ones, b))[0:8])
@@ -765,8 +818,8 @@
         out_specs=(vmem, vmem),
         scratch_shapes=[
             dma((4,)),
-            dma((8,)),
-            dma((8,)),
+            dma((3,)),
+            dma((3,)),
         ],
         compiler_params=pltpu.CompilerParams(
             collective_id=0, has_side_effects=True, vmem_limit_bytes=8 * 1024 * 1024
@@ -790,7 +843,7 @@
         pltpu.VMEM((2 * cz * cy, 3 * cx), bf16),
         pltpu.VMEM((kk * nmark, 2 * cz * cy), bf16),
         pltpu.VMEM((kk * nmark, cx), f32),
-        pltpu.VMEM((kk * nmark, 3 * cx), f32),
+        pltpu.VMEM((2, kk * nmark, 3 * cx), f32),
         pltpu.VMEM((nmark, ng1 * lane_count), bf16),
         pltpu.VMEM((nxc, 2 * rows, cx), f32),
         pltpu.VMEM((nxc, 2 * rows, cx), f32),
@@ -801,10 +854,8 @@
         pltpu.VMEM((ng1, 3, lane_count), f32),
         pltpu.VMEM((ng1, 3, lane_count), f32),
         pltpu.VMEM((ng2, 3, lane_count), f32),
-        dma((9,)),
-        dma((9,)),
-        dma((8,)),
-        dma((8,)),
+        dma((6,)),
+        dma((6,)),
         dma((2,)),
         dma((2,)),
         dma((2,)),

time: 49.6 us -> 48.4 us (0.976)
  Pallas kernels: 48.8 us -> 47.6 us
    pallas_call x1, Pallas kernels: 33.5 us -> 32.4 us  [local(): pl.pallas_call(functools.partial(step_kernel, split), out_shape=(pltpu.VM...]
where the time goes in v5:
time: 48.4 us; the launch traced here: 48.3 us
  Pallas kernels  47.6 us (98%)
  between operations  0.69 us (1%)
    pallas_call x1, Pallas kernels, local(): pl.pallas_call(functools.partial(step_kernel, split), out_shape=(pltpu.VM...  32.4 us
    pallas_call x1, Pallas kernels, local(): pl.pallas_call(functools.partial(velocity_kernel, split), out_shape=(pltp...  13.7 us
    pallas_call x1, Pallas kernels, local(): pl.pallas_call(write_kernel, out_shape=(jax.ShapeDtypeStruct((nq, cz, cy,...  1.5 us

profile of v5, /device:TPU:1, one launch (start us, length us, event | category | flops | bytes accessed | tf_op | source)
XLA Modules:
  0.0 48.3 jit_solution(8439049797550004878)
XLA Ops:
  0.6 0.0 copy-start.2
  0.6 0.0 copy-start.1
  0.7 0.0 copy-start
  0.7 13.7 %shard_map.67 = (f32[3,20,48,128]{3,2,1,0:T(8,128)S(1)}, bf16[19,16,32,128]{3,2,1,0:T(8,128)(2,1)S(1)}) custom-call(bf16[19,16,32,128]{3,2,1,0:T(8,128)(2,1)} %pops_hbm.1), custom_call_target="tpu_custom_call" | custom-call | tf_op jit(solution)/shard_map/pallas_call | solution.py:811
  14.4 0.0 copy-done.2
  14.4 0.0 copy-done.1
  14.4 0.0 copy-done
  14.4 32.4 %shard_map.68 = (bf16[19,16,32,128]{3,2,1,0:T(8,128)(2,1)S(1)}, f32[32,128]{1,0:T(8,128)S(1)}, f32[3,8]{1,0:T(4,128)S(1)}) custom-call(f32[3,20,48,128]{3,2,1,0:T(8,128)S(1)} %get-tuple-element.8.vel, bf16[19,16,32,128]{3,2,1,0:T(8,128)(2,1)S(1)} %get-tuple-element.9.pops, s32[8,128]{1,0:T(8,128)S(1)} %bitcast.2, f32[8,128]{1,0:T(8,128)S(1)} %bitcast.3, ...), custom_call_target="tpu_custom_call" | custom-call | tf_op jit(solution)/shard_map/pallas_call | solution.py:867
  46.8 1.5 %shard_map.69 = (bf16[19,16,32,128]{3,2,1,0:T(8,128)(2,1)}, f32[32,128]{1,0:T(8,128)}, f32[3,8]{1,0:T(4,128)}) custom-call(bf16[19,16,32,128]{3,2,1,0:T(8,128)(2,1)S(1)} %get-tuple-element.10.outv, f32[32,128]{1,0:T(8,128)S(1)} %get-tuple-element.11.eddy, f32[3,8]{1,0:T(4,128)S(1)} %get-tuple-element.12.force), custom_call_target="tpu_custom_call" | custom-call | tf_op jit(solution)/shard_map/pallas_call | solution.py:881
Async XLA Ops:
  0.6 13.7 %copy-start.2 = (s32[128]{0:T(128)S(1)}, s32[128]{0:T(128)}, u32[]{:S(2)}) copy-start(s32[128]{0:T(128)} %seg_ref.1) | copy-start | bytes 1540
  0.6 13.7 %copy-start.1 = (f32[128,8]{0,1:T(8,128)S(1)}, f32[128,8]{0,1:T(8,128)}, u32[]{:S(2)}) copy-start(f32[128,8]{0,1:T(8,128)} %param.6) | copy-start | bytes 12292
  0.7 13.7 %copy-start = (s32[128,8]{0,1:T(8,128)S(1)}, s32[128,8]{0,1:T(8,128)}, u32[]{:S(2)}) copy-start(s32[128,8]{0,1:T(8,128)} %param.5) | copy-start | bytes 12292
